TPU v7x, 32 devices: a whole 2x2x4 slice. The times are simulated.
32 devices in a mesh: groups: 2 (over x), row: 16 (over z, y, core).
Axes of the slice: x: 2, y: 2, z: 4, core: 2. Of those that a mesh axis runs over, the one named last changes fastest.
Arguments:
- object_field: float32 [2, 8192, 512], P(None, ('groups', 'row')), parts along dimension 1, may hold values from -5 to 5
- probe_wave: float32 [2, 512, 256], P(None, 'groups'), parts along dimension 1, may hold values from -5 to 5
- patterns: float32 [256, 256, 256], P(('groups', 'row')), parts along dimension 0, may hold values from 0.1 to 4
- positions: int32 [256, 2], P(('groups', 'row')), parts along dimension 0, may hold values from -128 to 3967, as said below
- counts: int32 [32], P('groups'), parts along dimension 0, may hold values from 1 to 8, as said below
Outputs:
- object_grad: float32 [2, 8192, 512], P(None, ('groups', 'row')), parts along dimension 1
- probe_grad: float32 [2, 512, 256], P(None, 'groups'), parts along dimension 1
There are 2 independent parts, one for each index of `groups`. A program takes and returns all parts, laid end to end along the dimension named above; each array names one. Nothing has to cross between parts.
Inputs may be any that keep to these rules, and one draw needn't show every extreme that they name: The live slots of tile t are its first counts[t] slots; some tile has all 8 live. The patch of slot j has its centre row positions[j, 0] + 128 inside tile j // 8 (object rows (j // 8) * 256 to that plus 256 - 1); its corner column lies in 0 to 256.
All inputs are finite; a program needn't handle non-finite values.
Results may differ from a plain program's by a relative error of at most 0.0003.
Values sent between devices are 32-bit elements; how exact they have to be, the bound alone decides.
A program may use at most 64 MiB of HBM per device.

v0:
```python
import math

import jax
import jax.numpy as jnp
from jax import lax
from jax.sharding import PartitionSpec as P


def extended(block, sides, width):
    for axis, dim in sides:
        count = lax.axis_size(axis)
        forward = [(i, i + 1) for i in range(count - 1)]
        backward = [(target, source) for source, target in forward]
        low = lax.ppermute(
            lax.slice_in_dim(block, block.shape[dim] - width, None, axis=dim), axis, forward
        )
        high = lax.ppermute(lax.slice_in_dim(block, 0, width, axis=dim), axis, backward)
        block = jnp.concatenate([low, block, high], axis=dim)
    return block


def passed_along(value, axis, steps):
    count = lax.axis_size(axis)
    leading, last = (max(0, -steps), min(count, count - steps))
    return lax.ppermute(value, axis, [(source, source + steps) for source in range(leading, last)])


def dft_tables(extent):
    index_line = jnp.arange(extent, dtype=jnp.int32)
    phase = index_line[:, None] * index_line[None, :] % extent
    angle = phase.astype(jnp.float32) * (2.0 * math.pi / extent)
    factor = 1.0 / math.sqrt(extent)
    return (jnp.cos(angle) * factor, -jnp.sin(angle) * factor)


def matmul(left, right):
    return jnp.dot(left, right, precision=lax.Precision.HIGHEST, preferred_element_type=jnp.float32)


def complex_product(left_re, left_im, right_re, right_im):
    return (
        matmul(left_re, right_re) - matmul(left_im, right_im),
        matmul(left_re, right_im) + matmul(left_im, right_re),
    )


def far_field(wave_re, wave_im, pattern, cos_table, sin_table):
    half_re, half_im = complex_product(cos_table, sin_table, wave_re, wave_im)
    spec_re, spec_im = complex_product(half_re, half_im, cos_table, sin_table)
    misfit = spec_re * spec_re + spec_im * spec_im - pattern
    back_re, back_im = complex_product(cos_table, -sin_table, misfit * spec_re, misfit * spec_im)
    return complex_product(back_re, back_im, cos_table, -sin_table)


def local(object_field, probe_wave, patterns, positions, counts):
    tile_rows = object_field.shape[1]
    extent = probe_wave.shape[1]
    half_width = extent // 2
    my_index = lax.axis_index("row")
    my_count = lax.dynamic_index_in_dim(counts, my_index, 0, keepdims=False)
    padded = extended(object_field, (("row", 1),), half_width)
    row_base = my_index * tile_rows
    cos_table, sin_table = dft_tables(extent)
    anchor = jnp.zeros((), jnp.int32)

    def patch_at(slot_index):
        corner = lax.dynamic_index_in_dim(positions, slot_index, 0, keepdims=False)
        starts = (anchor, corner[0] - row_base + half_width, corner[1])
        return (lax.dynamic_slice(padded, starts, (2, extent, extent)), starts)

    def exit_wave(patch):
        wave_re = probe_wave[0] * patch[0] - probe_wave[1] * patch[1]
        wave_im = probe_wave[0] * patch[1] + probe_wave[1] * patch[0]
        return (wave_re, wave_im)

    def add_gradient(totals, patch, starts, grad_re, grad_im):
        object_total, probe_total = totals
        object_re = probe_wave[0] * grad_re + probe_wave[1] * grad_im
        object_im = probe_wave[0] * grad_im - probe_wave[1] * grad_re
        current = lax.dynamic_slice(object_total, starts, (2, extent, extent))
        object_total = lax.dynamic_update_slice(
            object_total, current + jnp.stack([object_re, object_im]), starts
        )
        probe_re = patch[0] * grad_re + patch[1] * grad_im
        probe_im = patch[0] * grad_im - patch[1] * grad_re
        return (object_total, probe_total + jnp.stack([probe_re, probe_im]))

    def full_step(slot_index, totals):
        patch, starts = patch_at(slot_index)
        wave_re, wave_im = exit_wave(patch)
        pattern = lax.dynamic_index_in_dim(patterns, slot_index, 0, keepdims=False)
        grad_re, grad_im = far_field(wave_re, wave_im, pattern, cos_table, sin_table)
        return add_gradient(totals, patch, starts, grad_re, grad_im)

    totals = (jnp.zeros(padded.shape, jnp.float32), jnp.zeros(probe_wave.shape, jnp.float32))
    totals = lax.fori_loop(0, my_count, full_step, totals)
    object_total, probe_total = totals
    from_below = passed_along(object_total[:, :half_width], "row", -1)
    from_above = passed_along(object_total[:, half_width + tile_rows :], "row", 1)
    own_rows = object_total[:, half_width : half_width + tile_rows]
    own_rows = own_rows.at[:, :half_width].add(from_above)
    own_rows = own_rows.at[:, tile_rows - half_width :].add(from_below)
    probe_grad = lax.psum(probe_total, "row")
    return (own_rows, probe_grad)


def solution(mesh):
    placed = (
        P(None, ("groups", "row"), None),
        P(None, "groups", None),
        P(("groups", "row"), None, None),
        P(("groups", "row"), None),
        P("groups"),
    )
    return jax.shard_map(
        local,
        mesh=mesh,
        in_specs=placed,
        out_specs=(P(None, ("groups", "row"), None), P(None, "groups", None)),
        check_vma=False,
    )
```

profile of v0, /device:TPU:1, one launch (start us, length us, event | category | flops | bytes accessed | tf_op | source)
XLA Modules:
  0.0 449.5 jit_solution(1090874234785577451)
XLA Ops:
  8.6 4.5 %collective-permute-start = (f32[2,128,512]{2,1,0:T(8,128)S(1)}, f32[2,128,512]{2,1,0:T(8,128)S(1)}, u32[]{:S(2)}, u32[]{:S(2)}) collective-permute-start(f32[2,128,512]{2,1,0:T(8,128)S(1)} %get-tuple-element.316), channel_id=1, source_target_pairs={{0,1},{1,2},{2,3},{3,4},{4,5},{5,6},{6,7},{7,8},{8,9},{9,10},{10,1... | collective-permute-start | bytes 1572872 | tf_op jit(solution)/shard_map/ppermute | solution.py:14
  13.1 1.9 collective-permute-start.1
  15.7 9.1 %collective-permute-done = f32[2,128,512]{2,1,0:T(8,128)S(1)} collective-permute-done((f32[2,128,512]{2,1,0:T(8,128)S(1)}, f32[2,128,512]{2,1,0:T(8,128)S(1)}, u32[]{:S(2)}, u32[]{:S(2)}) %collective-permute-start) | collective-permute-done | bytes 524320 | tf_op jit(solution)/shard_map/ppermute | solution.py:14
  29.5 301.4 %while.18 = (s32[]{:T(128)}, f32[2,512,512]{2,1,0:T(8,128)}, f32[2,256,256]{2,1,0:T(8,128)}, s32[]{:T(128)}, s32[8,2]{0,1:T(2,128)S(1)}, /*index=5*/s32[]{:T(128...) while((s32[]{:T(128)}, f32[2,512,512]{2,1,0:T(8,128)}, ...), condition=%wide.region_1.2_spmd.clone.clone, body=%wide.region_0.1_spmd.clone.clone.sunk | while | flops 3240361984 | bytes 23331244 | solution.py:96
  43.9 2.4 fusion.191
  60.6 6.2 %dynamic_update_slice.9 = f32[2,512,512]{2,1,0:T(8,128)} dynamic-update-slice(f32[2,512,512]{2,1,0:T(8,128)} %get-tuple-element.415, f32[2,256,256]{2,1,0:T(8,128)S(1)} %get-tuple-element.396, s32[]{:T(128)} %constant.114.clone.1..sunk, s32[]{:T(128)S(6)} %select_n.159, s32[]{:T(128)S(6)} %select_n.160) | dynamic-update-slice | bytes 1048580 | tf_op jit(solution)/shard_map/while/body/dynamic_update_slice | solution.py:81
  81.3 2.4 fusion.191
  98.0 6.6 %dynamic_update_slice.9 = f32[2,512,512]{2,1,0:T(8,128)} dynamic-update-slice(f32[2,512,512]{2,1,0:T(8,128)} %get-tuple-element.415, f32[2,256,256]{2,1,0:T(8,128)S(1)} %get-tuple-element.396, s32[]{:T(128)} %constant.114.clone.1..sunk, s32[]{:T(128)S(6)} %select_n.159, s32[]{:T(128)S(6)} %select_n.160) | dynamic-update-slice | bytes 1048580 | tf_op jit(solution)/shard_map/while/body/dynamic_update_slice | solution.py:81
  119.1 2.4 fusion.191
  135.9 6.4 %dynamic_update_slice.9 = f32[2,512,512]{2,1,0:T(8,128)} dynamic-update-slice(f32[2,512,512]{2,1,0:T(8,128)} %get-tuple-element.415, f32[2,256,256]{2,1,0:T(8,128)S(1)} %get-tuple-element.396, s32[]{:T(128)} %constant.114.clone.1..sunk, s32[]{:T(128)S(6)} %select_n.159, s32[]{:T(128)S(6)} %select_n.160) | dynamic-update-slice | bytes 1048580 | tf_op jit(solution)/shard_map/while/body/dynamic_update_slice | solution.py:81
  156.7 2.4 fusion.191
  173.5 5.9 %dynamic_update_slice.9 = f32[2,512,512]{2,1,0:T(8,128)} dynamic-update-slice(f32[2,512,512]{2,1,0:T(8,128)} %get-tuple-element.415, f32[2,256,256]{2,1,0:T(8,128)S(1)} %get-tuple-element.396, s32[]{:T(128)} %constant.114.clone.1..sunk, s32[]{:T(128)S(6)} %select_n.159, s32[]{:T(128)S(6)} %select_n.160) | dynamic-update-slice | bytes 1048580 | tf_op jit(solution)/shard_map/while/body/dynamic_update_slice | solution.py:81
  193.8 2.4 fusion.191
  210.5 6.7 %dynamic_update_slice.9 = f32[2,512,512]{2,1,0:T(8,128)} dynamic-update-slice(f32[2,512,512]{2,1,0:T(8,128)} %get-tuple-element.415, f32[2,256,256]{2,1,0:T(8,128)S(1)} %get-tuple-element.396, s32[]{:T(128)} %constant.114.clone.1..sunk, s32[]{:T(128)S(6)} %select_n.159, s32[]{:T(128)S(6)} %select_n.160) | dynamic-update-slice | bytes 1048580 | tf_op jit(solution)/shard_map/while/body/dynamic_update_slice | solution.py:81
  231.7 2.4 fusion.191
  248.4 6.4 %dynamic_update_slice.9 = f32[2,512,512]{2,1,0:T(8,128)} dynamic-update-slice(f32[2,512,512]{2,1,0:T(8,128)} %get-tuple-element.415, f32[2,256,256]{2,1,0:T(8,128)S(1)} %get-tuple-element.396, s32[]{:T(128)} %constant.114.clone.1..sunk, s32[]{:T(128)S(6)} %select_n.159, s32[]{:T(128)S(6)} %select_n.160) | dynamic-update-slice | bytes 1048580 | tf_op jit(solution)/shard_map/while/body/dynamic_update_slice | solution.py:81
  269.2 2.4 fusion.191
  286.0 6.5 %dynamic_update_slice.9 = f32[2,512,512]{2,1,0:T(8,128)} dynamic-update-slice(f32[2,512,512]{2,1,0:T(8,128)} %get-tuple-element.415, f32[2,256,256]{2,1,0:T(8,128)S(1)} %get-tuple-element.396, s32[]{:T(128)} %constant.114.clone.1..sunk, s32[]{:T(128)S(6)} %select_n.159, s32[]{:T(128)S(6)} %select_n.160) | dynamic-update-slice | bytes 1048580 | tf_op jit(solution)/shard_map/while/body/dynamic_update_slice | solution.py:81
  306.9 2.4 fusion.191
  323.6 6.7 %dynamic_update_slice.9 = f32[2,512,512]{2,1,0:T(8,128)} dynamic-update-slice(f32[2,512,512]{2,1,0:T(8,128)} %get-tuple-element.415, f32[2,256,256]{2,1,0:T(8,128)S(1)} %get-tuple-element.396, s32[]{:T(128)} %constant.114.clone.1..sunk, s32[]{:T(128)S(6)} %select_n.159, s32[]{:T(128)S(6)} %select_n.160) | dynamic-update-slice | bytes 1048580 | tf_op jit(solution)/shard_map/while/body/dynamic_update_slice | solution.py:81
  332.2 4.8 %collective-permute-start.2 = (f32[2,128,512]{2,1,0:T(8,128)S(1)}, f32[2,128,512]{2,1,0:T(8,128)S(1)}, u32[]{:S(2)}, u32[]{:S(2)}) collective-permute-start(f32[2,128,512]{2,1,0:T(8,128)S(1)} %slice.118), channel_id=1, source_target_pairs={{0,1},{1,2},{2,3},{3,4},{4,5},{5,6},{6,7},{7,8},{8,9},{9,10},{10,1... | collective-permute-start | bytes 1572872 | tf_op jit(solution)/shard_map/ppermute | solution.py:25
  338.3 4.8 %collective-permute-done.2 = f32[2,128,512]{2,1,0:T(8,128)S(1)} collective-permute-done((f32[2,128,512]{2,1,0:T(8,128)S(1)}, f32[2,128,512]{2,1,0:T(8,128)S(1)}, u32[]{:S(2)}, u32[]{:S(2)}) %collective-permute-start.2) | collective-permute-done | bytes 524320 | tf_op jit(solution)/shard_map/ppermute | solution.py:25
  345.2 9.3 %collective-permute-done.3 = f32[2,128,512]{2,1,0:T(8,128)S(1)} collective-permute-done((f32[2,128,512]{2,1,0:T(8,128)S(1)}, f32[2,128,512]{2,1,0:T(8,128)S(1)}, u32[]{:S(2)}, u32[]{:S(2)}) %collective-permute-start.3) | collective-permute-done | bytes 524320 | tf_op jit(solution)/shard_map/ppermute | solution.py:25
  354.6 86.2 %all-reduce.2.cloned.1.call-done = f32[2,256,256]{2,1,0:T(8,128)} async-done(((f32[2,256,256]{2,1,0:T(8,128)}), f32[2,256,256]{2,1,0:T(8,128)}) %all-reduce.2.cloned.1.call-update) | async-done | bytes 524304 | tf_op jit(solution)/shard_map/psum | solution.py:103
  (212 shorter events, 216.2 us)
Async XLA Ops:
  7.2 18.5 %copy-start.4 = (f32[2,256,512]{2,1,0:T(8,128)S(1)}, f32[2,256,512]{2,1,0:T(8,128)}, u32[]{:S(2)}) copy-start(f32[2,256,512]{2,1,0:T(8,128)} %param.11) | copy-start | bytes 3145732
  7.2 7.9 %copy-start.8 = (s32[16]{0:T(128)S(1)}, s32[16]{0:T(128)}, u32[]{:S(2)}) copy-start(s32[16]{0:T(128)} %param.15) | copy-start | bytes 196
  7.2 433.6 %all-reduce.2.cloned.1.call-start = ((), (), s32[]{:S(2)}) async-start(), calls=%async_computation | async-start | bytes 1048576 | tf_op jit(solution)/shard_map/psum | solution.py:103
  8.6 16.3 %collective-permute-start = (f32[2,128,512]{2,1,0:T(8,128)S(1)}, f32[2,128,512]{2,1,0:T(8,128)S(1)}, u32[]{:S(2)}, u32[]{:S(2)}) collective-permute-start(f32[2,128,512]{2,1,0:T(8,128)S(1)} %get-tuple-element.316), channel_id=1, source_target_pairs={{0,1},{1,2},{2,3},{3,4},{4,5},{5,6},{6,7},{7,8},{8,9},{9,10},{10,1... | collective-permute-start | bytes 1572872 | tf_op jit(solution)/shard_map/ppermute | solution.py:14
  13.1 12.5 %collective-permute-start.1 = (f32[2,128,512]{2,1,0:T(8,128)S(1)}, f32[2,128,512]{2,1,0:T(8,128)}, u32[]{:S(2)}, u32[]{:S(2)}) collective-permute-start(f32[2,128,512]{2,1,0:T(8,128)S(1)} %get-tuple-element.317), channel_id=1, source_target_pairs={{1,0},{2,1},{3,2},{4,3},{5,4},{6,5},{7,6},{8,7},{9,8},{10,9},{11,1... | collective-permute-start | bytes 1572872 | tf_op jit(solution)/shard_map/ppermute | solution.py:17
  27.0 2.5 copy-start
  27.0 2.4 copy-start.7
  55.3 3.1 copy-start.2
  59.9 0.8 copy-start.3
  92.7 3.1 copy-start.2
  97.2 0.8 copy-start.3
  130.5 3.1 copy-start.2
  135.1 0.8 copy-start.3
  168.1 3.1 copy-start.2
  205.1 3.1 copy-start.2
  209.7 0.8 copy-start.3
  243.0 3.1 copy-start.2
  280.6 3.1 copy-start.2
  318.3 3.1 copy-start.2
  322.8 0.8 copy-start.3
  330.9 12.1 %copy-start.1 = (f32[2,512,512]{2,1,0:T(8,128)S(1)}, f32[2,512,512]{2,1,0:T(8,128)}, u32[]{:S(2)}) copy-start(f32[2,512,512]{2,1,0:T(8,128)} %get-tuple-element.212) | copy-start | bytes 6291460
  332.2 10.9 %collective-permute-start.2 = (f32[2,128,512]{2,1,0:T(8,128)S(1)}, f32[2,128,512]{2,1,0:T(8,128)S(1)}, u32[]{:S(2)}, u32[]{:S(2)}) collective-permute-start(f32[2,128,512]{2,1,0:T(8,128)S(1)} %slice.118), channel_id=1, source_target_pairs={{0,1},{1,2},{2,3},{3,4},{4,5},{5,6},{6,7},{7,8},{8,9},{9,10},{10,1... | collective-permute-start | bytes 1572872 | tf_op jit(solution)/shard_map/ppermute | solution.py:25
  343.2 11.2 %collective-permute-start.3 = (f32[2,128,512]{2,1,0:T(8,128)S(1)}, f32[2,128,512]{2,1,0:T(8,128)S(1)}, u32[]{:S(2)}, u32[]{:S(2)}) collective-permute-start(f32[2,128,512]{2,1,0:T(8,128)S(1)} %get-tuple-element.314), channel_id=1, source_target_pairs={{1,0},{2,1},{3,2},{4,3},{5,4},{6,5},{7,6},{8,7},{9,8},{10,9},{11,1... | collective-permute-start | bytes 1572872 | tf_op jit(solution)/shard_map/ppermute | solution.py:25
  354.6 88.1 %copy-start.5 = (f32[2,256,512]{2,1,0:T(8,128)}, f32[2,256,512]{2,1,0:T(8,128)S(1)}, u32[]{:S(2)}) copy-start(f32[2,256,512]{2,1,0:T(8,128)S(1)} %fusion.112) | copy-start | bytes 3145732
  (4 other events, 3.2 us)
Sparse Core Ops, SparseCore 0:
  345.3 95.4 all-reduce.1
where the time goes:
time: 450 us
  matrix products  197 us (44%)
  waiting for transfers between devices  109 us (24%)
  local copies, waits for them, and re-layouts  72.8 us (16%)
  loops' own time  27.7 us (6%)
  other arithmetic  15.4 us (3%)
  between operations  14.2 us (3%)
  starting transfers between devices  13.2 us (3%)
    dot_general x128, matrix products, matmul(): jnp.dot(left, right, precision=lax.Precision.HIGHEST, preferred_element_t...  197 us
    psum x1, waiting for transfers between devices, local(): probe_grad = lax.psum(probe_total, 'row')  86.2 us
    dynamic_update_slice x8, local copies, waits for them, and re-layouts, add_gradient(): lax.dynamic_update_slice(object_total, current + jnp.stack([object_re, ob...  51.4 us
    another operation x1, loops' own time, local(): totals = lax.fori_loop(0, my_count, full_step, totals)  27.7 us
    ppermute x2, waiting for transfers between devices, passed_along(): lax.ppermute(value, axis, [(source, source + steps) for source in range(l...  14.1 us
    add x8, other arithmetic, add_gradient(): current + jnp.stack([object_re, object_im])  12 us
    ppermute x1, waiting for transfers between devices, extended(): lax.ppermute(lax.slice_in_dim(block, block.shape[dim] - width, None, axis...  9.13 us
  transfers between devices with their start and end apart: 5, of which 4 were waited for; matrix products, arithmetic and copies ran while one was open for 0% of the time, Pallas kernels for 0%

commit v1 on v0

v1 whole, which is shorter than its diff:
```python
import functools
import math

import jax
import jax.numpy as jnp
import ml_dtypes
import numpy as np
from jax import lax
from jax.experimental import pallas as pl
from jax.experimental.pallas import tpu as pltpu
from jax.sharding import PartitionSpec as P

F32 = jnp.float32
BF16 = jnp.bfloat16


def tables(extent):
    half = extent // 2
    line = np.arange(half)
    out = []
    for parity in (0, 1):
        angle = ((2 * line[:, None] + parity) * line[None, :] % extent) * (2.0 * math.pi / extent)
        cos, sin = np.cos(angle) / math.sqrt(extent), np.sin(angle) / math.sqrt(extent)
        full = np.block([[cos, sin], [-sin, cos]])
        for matrix in (full, full.T):
            high = matrix.astype(ml_dtypes.bfloat16)
            low = (matrix - high.astype(np.float64)).astype(ml_dtypes.bfloat16)
            out += [high, low]
    order = np.zeros((extent, extent), np.float32)
    order[2 * line, line] = 1
    order[2 * line + 1, half + line] = 1
    out.append(order.astype(ml_dtypes.bfloat16))
    return np.stack(out)


def parts(value):
    high = value.astype(BF16)
    return high, (value - high.astype(F32)).astype(BF16)


def dot(left, right):
    return jnp.dot(left, right, preferred_element_type=F32)


def from_left(table, index, value):
    high, low = parts(value)
    return dot(
        jnp.concatenate([table[index], table[index], table[index + 1]], axis=1),
        jnp.concatenate([high, low, high], axis=0),
    )


def from_right(value, table, index):
    high, low = parts(value)
    return dot(
        jnp.concatenate([high, low, high], axis=1),
        jnp.concatenate([table[index], table[index], table[index + 1]], axis=0),
    )


def lanes(*blocks):
    return jnp.concatenate(blocks, axis=1)


def rows(*blocks):
    return jnp.concatenate(blocks, axis=0)


def transform(re, im, table):
    h = re.shape[0] // 2
    even = from_right(lanes(re[:, :h] + re[:, h:], im[:, :h] + im[:, h:]), table, 2)
    odd = from_right(lanes(re[:, :h] - re[:, h:], im[:, :h] - im[:, h:]), table, 6)
    re, im = lanes(even[:, :h], odd[:, :h]), lanes(even[:, h:], odd[:, h:])
    even = from_left(table, 0, rows(re[:h] + re[h:], im[:h] + im[h:]))
    odd = from_left(table, 4, rows(re[:h] - re[h:], im[:h] - im[h:]))
    return even, odd


def inverse(even, odd, table):
    h = even.shape[0] // 2
    total = from_left(table, 2, even)
    other = from_left(table, 6, odd)
    top, low = total + other, total - other
    even = from_right(rows(lanes(top[:h, :h], top[h:, :h]), lanes(low[:h, :h], low[h:, :h])), table, 0)
    odd = from_right(rows(lanes(top[:h, h:], top[h:, h:]), lanes(low[:h, h:], low[h:, h:])), table, 4)
    total, other = even + odd, even - odd
    return lanes(total[:, :h], other[:, :h]), lanes(total[:, h:], other[:, h:])


def misfit_kernel(
    corner, count, low, own, high, probe, patterns, table, grad_low, grad_own, grad_high, grad_probe, field, total, ordered
):
    extent = probe.shape[1]
    h = extent // 2
    tile = own.shape[1]
    field[:, :h] = low[...]
    field[:, h : h + tile] = own[...]
    field[:, h + tile :] = high[...]
    total[...] = jnp.zeros_like(total)
    grad_probe[...] = jnp.zeros_like(grad_probe)
    column = lax.broadcasted_iota(jnp.int32, (extent, extent), 1)

    def step(slot, carry):
        first = corner[2 * slot]
        shift = corner[2 * slot + 1]
        kept = column >= shift
        sub = lax.rem(first, 8)
        base = pl.multiple_of(first - sub, 8)
        at = pl.ds(base, extent)
        after = pl.ds(pl.multiple_of(base + extent, 8), 8)
        inside = lax.broadcasted_iota(jnp.int32, (8, extent), 0) >= sub

        def patch_of(i):
            body = jnp.where(kept, field[i, at, :extent], field[i, at, extent:])
            wrap = jnp.where(kept[:8], field[i, after, :extent], field[i, after, extent:])
            return rows(jnp.where(inside, body[:8], wrap), body[8:])

        patch = [patch_of(i) for i in (0, 1)]
        turned = [
            pltpu.roll(pltpu.roll(probe[i], lax.rem(shift, extent), 1), sub, 0) for i in (0, 1)
        ]
        even, odd = transform(
            turned[0] * patch[0] - turned[1] * patch[1], turned[0] * patch[1] + turned[1] * patch[0], table
        )
        permuted = dot(lanes(*parts(patterns[slot])), rows(table[8], table[8]))
        ordered[0] = permuted[:, :h]
        ordered[1] = permuted[:, h:]
        results = []
        for parity, value in ((0, even), (1, odd)):
            pattern = lanes(ordered[0, pl.ds(parity, h, 2), :], ordered[1, pl.ds(parity, h, 2), :])
            gap = value[:h] * value[:h] + value[h:] * value[h:] - pattern
            results.append(rows(gap * value[:h], gap * value[h:]))
        re, im = inverse(results[0], results[1], table)
        zero = jnp.zeros_like(re)
        grads = (turned[0] * re + turned[1] * im, turned[0] * im - turned[1] * re)
        for i in (0, 1):
            body = rows(jnp.where(inside, grads[i][:8], zero[:8]), grads[i][8:])
            wrap = jnp.where(inside, zero[:8], grads[i][:8])
            total[i, at, :extent] += jnp.where(kept, body, zero)
            total[i, at, extent:] += jnp.where(kept, zero, body)
            total[i, after, :extent] += jnp.where(kept[:8], wrap, zero[:8])
            total[i, after, extent:] += jnp.where(kept[:8], zero[:8], wrap)
        back = lax.rem(extent - lax.rem(shift, extent), extent)
        up = lax.rem(extent - sub, extent)
        for i, value in enumerate((patch[0] * re + patch[1] * im, patch[0] * im - patch[1] * re)):
            grad_probe[i] += pltpu.roll(pltpu.roll(value, back, 1), up, 0)
        return carry

    lax.fori_loop(0, count[0], step, 0)
    grad_low[...] = total[:, :h]
    grad_own[...] = total[:, h : h + tile]
    grad_high[...] = total[:, h + tile :]


def misfit_call(corner, count, low, own, high, probe, patterns, table):
    vmem = pl.BlockSpec(memory_space=pltpu.VMEM)
    smem = pl.BlockSpec(memory_space=pltpu.SMEM)
    height = low.shape[1] + own.shape[1] + high.shape[1]
    return pl.pallas_call(
        misfit_kernel,
        out_shape=(
            jax.ShapeDtypeStruct(low.shape, F32),
            jax.ShapeDtypeStruct(own.shape, F32),
            jax.ShapeDtypeStruct(high.shape, F32),
            jax.ShapeDtypeStruct(probe.shape, F32),
        ),
        in_specs=[smem, smem] + [vmem] * 6,
        out_specs=(vmem,) * 4,
        scratch_shapes=[pltpu.VMEM((2, height, own.shape[2]), F32)] * 2
        + [pltpu.VMEM((2, probe.shape[1], probe.shape[1] // 2), F32)],
        compiler_params=pltpu.CompilerParams(vmem_limit_bytes=48 * 1024 * 1024),
        name="misfit",
    )(corner, count, low, own, high, probe, patterns, table)


def passed_along(value, axis, steps):
    count = lax.axis_size(axis)
    leading, last = (max(0, -steps), min(count, count - steps))
    return lax.ppermute(value, axis, [(source, source + steps) for source in range(leading, last)])


def local(object_field, probe_wave, patterns, positions, counts):
    tile = object_field.shape[1]
    extent = probe_wave.shape[1]
    h = extent // 2
    me = lax.axis_index("row")
    count = lax.dynamic_slice(counts, (me,), (1,))
    low = passed_along(object_field[:, tile - h :], "row", 1)
    high = passed_along(object_field[:, :h], "row", -1)
    corner = (positions - jnp.stack([me * tile - h, 0 * me])[None]).reshape(-1)
    table = jnp.asarray(tables(extent))
    grad_low, grad_own, grad_high, grad_probe = misfit_call(
        corner, count, low, object_field, high, probe_wave, patterns, table
    )
    from_below = passed_along(grad_low, "row", -1)
    from_above = passed_along(grad_high, "row", 1)
    grad_own = grad_own + jnp.concatenate([from_above, from_below], axis=1)
    return grad_own, lax.psum(grad_probe, "row")


def solution(mesh):
    placed = (
        P(None, ("groups", "row"), None),
        P(None, "groups", None),
        P(("groups", "row"), None, None),
        P(("groups", "row"), None),
        P("groups"),
    )
    return jax.shard_map(
        local,
        mesh=mesh,
        in_specs=placed,
        out_specs=(P(None, ("groups", "row"), None), P(None, "groups", None)),
        check_vma=False,
    )
```

time: 450 us -> 157 us (0.35)
  matrix products: 197 us -> 0 us
  local copies, waits for them, and re-layouts: 72.8 us -> 7.46 us
  loops' own time: 27.7 us -> 0 us
  Pallas kernels: 0 us -> 22.4 us
  other arithmetic: 15.4 us -> 1.32 us
  waiting for transfers between devices: 109 us -> 99.8 us
    dot_general x128 -> x0, matrix products: 197 us -> none  [matmul(): jnp.dot(left, right, precision=lax.Precision.HIGHEST, preferred_element_t...]
    dynamic_update_slice x8 -> x0, local copies, waits for them, and re-layouts: 51.4 us -> none  [add_gradient(): lax.dynamic_update_slice(object_total, current + jnp.stack([object_re, ob...]
    another operation x1 -> x0, loops' own time: 27.7 us -> none  [local(): totals = lax.fori_loop(0, my_count, full_step, totals)]
    pallas_call x0 -> x1, Pallas kernels: none -> 22.4 us  [misfit_call(): pl.pallas_call(misfit_kernel, out_shape=(jax.ShapeDtypeStruct(low.shape,...]
    add x16 -> x1, other arithmetic: 13.8 us -> 1.18 us  [local(): grad_own = grad_own + jnp.concatenate([from_above, from_below], axis=1)]
    ppermute x2 -> x0, waiting for transfers between devices: 9.13 us -> none  [the longest x1 9.13 us: extended(): lax.ppermute(lax.slice_in_dim(block, block.shape[dim] - width, None, axis...]
    slice x11 -> x1, local copies, waits for them, and re-layouts: 8.66 us -> 2.2 us  [local(): high = passed_along(object_field[:, :h], 'row', -1)]
    ppermute x2 -> x0, starting transfers between devices: 6.46 us -> none  [the longest x1 4.54 us: extended(): lax.ppermute(lax.slice_in_dim(block, block.shape[dim] - width, None, axis...]
  transfers between devices with their start and end apart: 5 -> 5, of which waited for: 4 -> 5; matrix products, arithmetic and copies ran while one was open for 0% -> 1% of each run, Pallas kernels for 0% -> 0%
where the time goes in v1:
time: 157 us; the launch traced here: 156 us
  waiting for transfers between devices  99.8 us (64%)
  Pallas kernels  22.4 us (14%)
  between operations  14.1 us (9%)
  starting transfers between devices  10.8 us (7%)
  local copies, waits for them, and re-layouts  7.46 us (5%)
    psum x1, waiting for transfers between devices, local(): return (grad_own, lax.psum(grad_probe, 'row'))  80.8 us
    pallas_call x1, Pallas kernels, misfit_call(): pl.pallas_call(misfit_kernel, out_shape=(jax.ShapeDtypeStruct(low.shape,...  22.4 us
    ppermute x4, waiting for transfers between devices, passed_along(): lax.ppermute(value, axis, [(source, source + steps) for source in range(l...  19 us
    ppermute x4, starting transfers between devices, passed_along(): lax.ppermute(value, axis, [(source, source + steps) for source in range(l...  10.8 us
    unnamed x15, local copies, waits for them, and re-layouts  4.51 us
  transfers between devices with their start and end apart: 5, of which 5 were waited for; matrix products, arithmetic and copies ran while one was open for 1% of the time, Pallas kernels for 0%

profile of v1, /device:TPU:1, one launch (start us, length us, event | category | flops | bytes accessed | tf_op | source)
XLA Modules:
  0.0 156.0 jit_solution(3204107875338960377)
XLA Ops:
  7.2 0.0 all-reduce.2.cloned.1.call-start
  7.2 2.2 %fusion = (f32[2,128,512]{2,1,0:T(8,128)}, f32[2,128,512]{2,1,0:T(8,128)S(1)}) fusion(f32[2,256,512]{2,1,0:T(8,128)} %own.1), kind=kLoop, calls=%fused_computation.3 | loop fusion | bytes 2097152 | tf_op jit(solution)/shard_map/slice | solution.py:189
  9.4 2.0 %collective-permute-start.1 = (f32[2,128,512]{2,1,0:T(8,128)}, f32[2,128,512]{2,1,0:T(8,128)S(1)}, u32[]{:S(2)}, u32[]{:S(2)}) collective-permute-start(f32[2,128,512]{2,1,0:T(8,128)} %get-tuple-element.10), channel_id=1, source_target_pairs={{1,0},{2,1},{3,2},{4,3},{5,4},{6,5},{7,6},{8,7},{9,8},{10,9},{11,1... | collective-permute-start | bytes 1572872 | tf_op jit(solution)/shard_map/ppermute | solution.py:179
  11.4 4.5 %collective-permute-start = (f32[2,128,512]{2,1,0:T(8,128)S(1)}, f32[2,128,512]{2,1,0:T(8,128)S(1)}, u32[]{:S(2)}, u32[]{:S(2)}) collective-permute-start(f32[2,128,512]{2,1,0:T(8,128)S(1)} %get-tuple-element.11), channel_id=1, source_target_pairs={{0,1},{1,2},{2,3},{3,4},{4,5},{5,6},{6,7},{7,8},{8,9},{9,10},{10,1... | collective-permute-start | bytes 1572872 | tf_op jit(solution)/shard_map/ppermute | solution.py:179
  15.9 0.1 pad_add_fusion
  16.0 0.0 copy-done.5
  16.0 0.1 broadcast_subtract_fusion
  16.1 0.1 copy.9
  16.1 0.1 reshape.8.corner
  16.2 0.6 dynamic_slice.3.count
  16.8 4.2 %collective-permute-done.1.high = f32[2,128,512]{2,1,0:T(8,128)S(1)} collective-permute-done((f32[2,128,512]{2,1,0:T(8,128)}, f32[2,128,512]{2,1,0:T(8,128)S(1)}, u32[]{:S(2)}, u32[]{:S(2)}) %collective-permute-start.1) | collective-permute-done | bytes 524320 | tf_op jit(solution)/shard_map/ppermute | solution.py:179
  21.0 5.8 %collective-permute-done.low = f32[2,128,512]{2,1,0:T(8,128)S(1)} collective-permute-done((f32[2,128,512]{2,1,0:T(8,128)S(1)}, f32[2,128,512]{2,1,0:T(8,128)S(1)}, u32[]{:S(2)}, u32[]{:S(2)}) %collective-permute-start) | collective-permute-done | bytes 524320 | tf_op jit(solution)/shard_map/ppermute | solution.py:179
  26.8 0.8 copy-done.2
  27.6 1.0 copy-done.3
  28.7 22.4 %misfit.1 = (f32[2,128,512]{2,1,0:T(8,128)}, f32[2,256,512]{2,1,0:T(8,128)S(1)}, f32[2,128,512]{2,1,0:T(8,128)}, f32[2,256,256]{2,1,0:T(8,128)S(1)}) custom-call(s32[16]{0:T(128)S(1)} %reshape.8.corner, s32[1]{0:T(128)} %dynamic_slice.3.count, f32[2,128,512]{2,1,0:T(8,128)S(1)} %copy-done.3, f32[2,256,512]{2,1,0:T(8,128)S(1)} %copy-done, ...), custom_call_target="tpu_custom_call" | custom-call | tf_op jit(solution)/shard_map/misfit/pallas_call | solution.py:159
  51.1 0.8 copy-done.4
  51.9 2.0 %collective-permute-start.2 = (f32[2,128,512]{2,1,0:T(8,128)}, f32[2,128,512]{2,1,0:T(8,128)S(1)}, u32[]{:S(2)}, u32[]{:S(2)}) collective-permute-start(f32[2,128,512]{2,1,0:T(8,128)} %get-tuple-element.7), channel_id=1, source_target_pairs={{0,1},{1,2},{2,3},{3,4},{4,5},{5,6},{6,7},{7,8},{8,9},{9,10},{10,1... | collective-permute-start | bytes 1572872 | tf_op jit(solution)/shard_map/ppermute | solution.py:179
  53.9 2.3 %collective-permute-start.3 = (f32[2,128,512]{2,1,0:T(8,128)}, f32[2,128,512]{2,1,0:T(8,128)S(1)}, u32[]{:S(2)}, u32[]{:S(2)}) collective-permute-start(f32[2,128,512]{2,1,0:T(8,128)} %get-tuple-element.8), channel_id=1, source_target_pairs={{1,0},{2,1},{3,2},{4,3},{5,4},{6,5},{7,6},{8,7},{9,8},{10,9},{11,1... | collective-permute-start | bytes 1572872 | tf_op jit(solution)/shard_map/ppermute | solution.py:179
  56.3 0.0 all-reduce.2.cloned.1.call-update
  56.3 4.1 %collective-permute-done.2 = f32[2,128,512]{2,1,0:T(8,128)S(1)} collective-permute-done((f32[2,128,512]{2,1,0:T(8,128)}, f32[2,128,512]{2,1,0:T(8,128)S(1)}, u32[]{:S(2)}, u32[]{:S(2)}) %collective-permute-start.2) | collective-permute-done | bytes 524320 | tf_op jit(solution)/shard_map/ppermute | solution.py:179
  60.4 4.9 %collective-permute-done.3 = f32[2,128,512]{2,1,0:T(8,128)S(1)} collective-permute-done((f32[2,128,512]{2,1,0:T(8,128)}, f32[2,128,512]{2,1,0:T(8,128)S(1)}, u32[]{:S(2)}, u32[]{:S(2)}) %collective-permute-start.3) | collective-permute-done | bytes 524320 | tf_op jit(solution)/shard_map/ppermute | solution.py:179
  65.3 1.2 maximum_add_fusion
  66.4 80.8 %all-reduce.2.cloned.1.call-done = f32[2,256,256]{2,1,0:T(8,128)} async-done(((f32[2,256,256]{2,1,0:T(8,128)}), f32[2,256,256]{2,1,0:T(8,128)}) %all-reduce.2.cloned.1.call-update) | async-done | bytes 524304 | tf_op jit(solution)/shard_map/psum | solution.py:198
  147.3 1.9 %copy.11 = f32[2,256,256]{2,1,0:T(8,128)} copy(f32[2,256,256]{2,1,0:T(8,128)} %all-reduce.2.cloned.1.call-done) | data formatting | bytes 1048576
  (10 shorter events, 0.0 us)
Async XLA Ops:
  7.2 20.5 %copy-start = (f32[2,256,512]{2,1,0:T(8,128)S(1)}, f32[2,256,512]{2,1,0:T(8,128)}, u32[]{:S(2)}) copy-start(f32[2,256,512]{2,1,0:T(8,128)} %own.1) | copy-start | bytes 3145732
  7.2 8.8 %copy-start.5 = (s32[8,2]{0,1:T(2,128)S(1)}, s32[8,2]{0,1:T(2,128)}, u32[]{:S(2)}) copy-start(s32[8,2]{0,1:T(2,128)} %param.9) | copy-start | bytes 196
  7.2 9.1 %copy-start.6 = (s32[16]{0:T(128)S(1)}, s32[16]{0:T(128)}, u32[]{:S(2)}) copy-start(s32[16]{0:T(128)} %param.10) | copy-start | bytes 196
  7.2 20.4 %copy-start.1 = (f32[2,256,256]{2,1,0:T(8,128)S(1)}, f32[2,256,256]{2,1,0:T(8,128)}, u32[]{:S(2)}) copy-start(f32[2,256,256]{2,1,0:T(8,128)} %probe.1) | copy-start | bytes 1572868
  7.2 140.1 %all-reduce.2.cloned.1.call-start = ((), (), s32[]{:S(2)}) async-start(), calls=%async_computation | async-start | bytes 1048576 | tf_op jit(solution)/shard_map/psum | solution.py:198
  9.4 11.6 %collective-permute-start.1 = (f32[2,128,512]{2,1,0:T(8,128)}, f32[2,128,512]{2,1,0:T(8,128)S(1)}, u32[]{:S(2)}, u32[]{:S(2)}) collective-permute-start(f32[2,128,512]{2,1,0:T(8,128)} %get-tuple-element.10), channel_id=1, source_target_pairs={{1,0},{2,1},{3,2},{4,3},{5,4},{6,5},{7,6},{8,7},{9,8},{10,9},{11,1... | collective-permute-start | bytes 1572872 | tf_op jit(solution)/shard_map/ppermute | solution.py:179
  11.4 15.4 %collective-permute-start = (f32[2,128,512]{2,1,0:T(8,128)S(1)}, f32[2,128,512]{2,1,0:T(8,128)S(1)}, u32[]{:S(2)}, u32[]{:S(2)}) collective-permute-start(f32[2,128,512]{2,1,0:T(8,128)S(1)} %get-tuple-element.11), channel_id=1, source_target_pairs={{0,1},{1,2},{2,3},{3,4},{4,5},{5,6},{6,7},{7,8},{8,9},{9,10},{10,1... | collective-permute-start | bytes 1572872 | tf_op jit(solution)/shard_map/ppermute | solution.py:179
  26.8 0.8 copy-start.2
  27.6 1.0 copy-start.3
  51.1 0.8 copy-start.4
  51.9 8.5 %collective-permute-start.2 = (f32[2,128,512]{2,1,0:T(8,128)}, f32[2,128,512]{2,1,0:T(8,128)S(1)}, u32[]{:S(2)}, u32[]{:S(2)}) collective-permute-start(f32[2,128,512]{2,1,0:T(8,128)} %get-tuple-element.7), channel_id=1, source_target_pairs={{0,1},{1,2},{2,3},{3,4},{4,5},{5,6},{6,7},{7,8},{8,9},{9,10},{10,1... | collective-permute-start | bytes 1572872 | tf_op jit(solution)/shard_map/ppermute | solution.py:179
  53.9 11.3 %collective-permute-start.3 = (f32[2,128,512]{2,1,0:T(8,128)}, f32[2,128,512]{2,1,0:T(8,128)S(1)}, u32[]{:S(2)}, u32[]{:S(2)}) collective-permute-start(f32[2,128,512]{2,1,0:T(8,128)} %get-tuple-element.8), channel_id=1, source_target_pairs={{1,0},{2,1},{3,2},{4,3},{5,4},{6,5},{7,6},{8,7},{9,8},{10,9},{11,1... | collective-permute-start | bytes 1572872 | tf_op jit(solution)/shard_map/ppermute | solution.py:179
Sparse Core Ops, SparseCore 0:
  56.4 90.8 all-reduce.1

commit v2 on v1

--- a/solution.py
+++ b/solution.py
@@ -93,9 +93,9 @@
     extent = probe.shape[1]
     h = extent // 2
     tile = own.shape[1]
-    field[:, :h] = low[...]
     field[:, h : h + tile] = own[...]
-    field[:, h + tile :] = high[...]
+    field[:, :h] = jnp.where(count[1] > 0, low[...], jnp.zeros_like(low))
+    field[:, h + tile :] = jnp.where(count[2] > 0, high[...], jnp.zeros_like(high))
     total[...] = jnp.zeros_like(total)
     grad_probe[...] = jnp.zeros_like(grad_probe)
     column = lax.broadcasted_iota(jnp.int32, (extent, extent), 1)
@@ -173,10 +173,214 @@
     )(corner, count, low, own, high, probe, patterns, table)
 
 
-def passed_along(value, axis, steps):
-    count = lax.axis_size(axis)
-    leading, last = (max(0, -steps), min(count, count - steps))
-    return lax.ppermute(value, axis, [(source, source + steps) for source in range(leading, last)])
+def radices(count):
+    out = []
+    while count > 1:
+        out.append(4 if len(out) >= 2 and count % 4 == 0 else 2)
+        count //= out[-1]
+    return out
+
+
+def signal(peer):
+    pl.semaphore_signal(
+        pltpu.get_barrier_semaphore(), inc=1, device_id={"row": peer}, device_id_type=pl.DeviceIdType.MESH
+    )
+
+
+def remote(source, target, send, recv, peer):
+    return pltpu.make_async_remote_copy(
+        src_ref=source,
+        dst_ref=target,
+        send_sem=send,
+        recv_sem=recv,
+        device_id={"row": peer},
+        device_id_type=pl.DeviceIdType.MESH,
+    )
+
+
+def both_sides(me, count, action):
+    @pl.when(me > 0)
+    def _():
+        action(0)
+
+    @pl.when(me < count - 1)
+    def _():
+        action(1)
+
+
+def neighbours(me, count):
+    return lax.min(me, 1) + lax.min(count - 1 - me, 1)
+
+
+def border_kernel(count, own, low, high, send, recv):
+    me = lax.axis_index("row")
+    h = low.shape[1]
+    up, down = lax.max(me - 1, 0), lax.min(me + 1, count - 1)
+    copies = (
+        remote(own.at[:, :h], high, send.at[0], recv.at[1], up),
+        remote(own.at[:, own.shape[1] - h :], low, send.at[1], recv.at[0], down),
+    )
+    arrivals = (
+        remote(own.at[:, :h], low, send.at[0], recv.at[0], up),
+        remote(own.at[:, :h], high, send.at[1], recv.at[1], down),
+    )
+    both_sides(me, count, lambda side: signal((up, down)[side]))
+    pl.semaphore_wait(pltpu.get_barrier_semaphore(), neighbours(me, count))
+    both_sides(me, count, lambda side: copies[side].start())
+    both_sides(me, count, lambda side: arrivals[side].wait_recv())
+    both_sides(me, count, lambda side: copies[side].wait_send())
+
+
+def border_call(own, h, count):
+    anywhere = pl.BlockSpec(memory_space=pl.ANY)
+    side = jax.ShapeDtypeStruct((own.shape[0], h, own.shape[2]), F32)
+    return pl.pallas_call(
+        functools.partial(border_kernel, count),
+        out_shape=(side, side),
+        in_specs=[anywhere],
+        out_specs=(anywhere, anywhere),
+        scratch_shapes=[pltpu.SemaphoreType.DMA((2,)), pltpu.SemaphoreType.DMA((2,))],
+        compiler_params=pltpu.CompilerParams(collective_id=0, has_side_effects=True),
+        name="border",
+    )(own)
+
+
+def sums_kernel(count, grad_low, grad_own, grad_high, probe, out, out_probe, from_above, from_below, *scratch):
+    me = lax.axis_index("row")
+    h = grad_low.shape[1]
+    tile = grad_own.shape[1]
+    steps = radices(count)
+    halo_send, halo_recv, rs_send, rs_recv, ag_send, ag_recv = scratch[:6]
+    held = scratch[6 : 6 + len(steps)]
+    landed = scratch[6 + len(steps) :]
+    up, down = lax.max(me - 1, 0), lax.min(me + 1, count - 1)
+
+    levels = []
+    stride, size, start = 1, probe.shape[0], 0
+    index = 0
+    for radix in steps:
+        digit = lax.rem(me // stride, radix)
+        size //= radix
+        others = []
+        for k in range(1, radix):
+            other = lax.rem(digit + k, radix)
+            others.append((index, k, other, me + (other - digit) * stride))
+            index += 1
+        levels.append((radix, digit, size, start, others))
+        start = start + digit * size
+        stride *= radix
+
+    both_sides(me, count, lambda side: signal((up, down)[side]))
+    for level in levels:
+        for _, _, _, peer in level[4]:
+            signal(peer)
+    pl.semaphore_wait(pltpu.get_barrier_semaphore(), index + neighbours(me, count))
+
+    halos = (
+        remote(grad_low, from_below, halo_send.at[0], halo_recv.at[1], up),
+        remote(grad_high, from_above, halo_send.at[1], halo_recv.at[0], down),
+    )
+    arrivals = (
+        remote(grad_low, from_above, halo_send.at[0], halo_recv.at[0], up),
+        remote(grad_high, from_below, halo_send.at[1], halo_recv.at[1], down),
+    )
+
+    def rs_copies(depth):
+        radix, digit, size, _, others = levels[depth]
+        source = probe if depth == 0 else held[depth - 1]
+        return [
+            remote(
+                source.at[pl.ds(pl.multiple_of(other * size, 8), size)],
+                landed[depth].at[radix - 1 - k],
+                rs_send.at[i],
+                rs_recv.at[levels[depth][4][radix - 1 - k][0]],
+                peer,
+            )
+            for i, k, other, peer in others
+        ]
+
+    def rs_arrivals(depth):
+        radix, digit, size, _, others = levels[depth]
+        source = probe if depth == 0 else held[depth - 1]
+        return [
+            remote(source.at[pl.ds(0, size)], landed[depth].at[k - 1], rs_send.at[i], rs_recv.at[i], peer)
+            for i, k, other, peer in others
+        ]
+
+    started = []
+    for depth, (radix, digit, size, _, others) in enumerate(levels):
+        copies = rs_copies(depth)
+        for copy in copies:
+            copy.start()
+        started += copies
+        if depth == 0:
+            both_sides(me, count, lambda side: halos[side].start())
+        source = probe if depth == 0 else held[depth - 1]
+        value = source[pl.ds(pl.multiple_of(digit * size, 8), size)]
+        for k, arrival in enumerate(rs_arrivals(depth)):
+            arrival.wait_recv()
+            value = value + landed[depth][k]
+        held[depth][...] = value
+
+    mine = pl.ds(pl.multiple_of(start, 8), levels[-1][2])
+    out_probe[mine] = held[-1][...]
+    for depth in reversed(range(len(levels))):
+        radix, digit, size, first, others = levels[depth]
+        region = pl.ds(pl.multiple_of(first + digit * size, 8), size)
+        copies = [
+            remote(
+                out_probe.at[region],
+                out_probe.at[region],
+                ag_send.at[i],
+                ag_recv.at[others[radix - 1 - k][0]],
+                peer,
+            )
+            for i, k, other, peer in others
+        ]
+        for copy in copies:
+            copy.start()
+        started += copies
+        for i, k, other, peer in others:
+            theirs = pl.ds(pl.multiple_of(first + other * size, 8), size)
+            remote(out_probe.at[region], out_probe.at[theirs], ag_send.at[i], ag_recv.at[i], peer).wait_recv()
+
+    out[...] = grad_own[...]
+
+    def add_side(side):
+        arrivals[side].wait_recv()
+        where, value = ((slice(0, h), from_above), (slice(tile - h, tile), from_below))[side]
+        out[:, where] += value[...]
+
+    both_sides(me, count, add_side)
+    for copy in started:
+        copy.wait_send()
+    both_sides(me, count, lambda side: halos[side].wait_send())
+
+
+def sums_call(grad_low, grad_own, grad_high, probe, count):
+    vmem = pl.BlockSpec(memory_space=pltpu.VMEM)
+    steps = radices(count)
+    pieces = sum(radix - 1 for radix in steps)
+    held, landed, size = [], [], probe.shape[0]
+    for radix in steps:
+        size //= radix
+        held.append(pltpu.VMEM((size, probe.shape[1]), F32))
+        landed.append(pltpu.VMEM((radix - 1, size, probe.shape[1]), F32))
+    return pl.pallas_call(
+        functools.partial(sums_kernel, count),
+        out_shape=(jax.ShapeDtypeStruct(grad_own.shape, F32), jax.ShapeDtypeStruct(probe.shape, F32)),
+        in_specs=[vmem] * 4,
+        out_specs=(vmem, vmem),
+        scratch_shapes=[pltpu.VMEM(grad_low.shape, F32)] * 2
+        + [pltpu.SemaphoreType.DMA((2,))] * 2
+        + [pltpu.SemaphoreType.DMA((pieces,))] * 4
+        + held
+        + landed,
+        compiler_params=pltpu.CompilerParams(
+            collective_id=1, has_side_effects=True, vmem_limit_bytes=40 * 1024 * 1024
+        ),
+        name="sums",
+    )(grad_low, grad_own, grad_high, probe)
 
 
 def local(object_field, probe_wave, patterns, positions, counts):
@@ -184,18 +388,17 @@
     extent = probe_wave.shape[1]
     h = extent // 2
     me = lax.axis_index("row")
+    size = lax.axis_size("row")
     count = lax.dynamic_slice(counts, (me,), (1,))
-    low = passed_along(object_field[:, tile - h :], "row", 1)
-    high = passed_along(object_field[:, :h], "row", -1)
+    low, high = border_call(object_field, h, size)
     corner = (positions - jnp.stack([me * tile - h, 0 * me])[None]).reshape(-1)
+    setup = jnp.concatenate([count, jnp.stack([me > 0, me < size - 1]).astype(jnp.int32)])
     table = jnp.asarray(tables(extent))
     grad_low, grad_own, grad_high, grad_probe = misfit_call(
-        corner, count, low, object_field, high, probe_wave, patterns, table
-    )
-    from_below = passed_along(grad_low, "row", -1)
-    from_above = passed_along(grad_high, "row", 1)
-    grad_own = grad_own + jnp.concatenate([from_above, from_below], axis=1)
-    return grad_own, lax.psum(grad_probe, "row")
+        corner, setup, low, object_field, high, probe_wave, patterns, table
+    )
+    grads, total = sums_call(grad_low, grad_own, grad_high, grad_probe.reshape(-1, extent), size)
+    return grads, total.reshape(grad_probe.shape)
 
 
 def solution(mesh):

time: 157 us -> 76.8 us (0.49)
  the two profiles are of different devices: /device:TPU:1 before, /device:TPU:7 now
where the time goes in v2:
time: 76.8 us; the launch traced here: 76 us
  Pallas kernels  66.2 us (86%)
  local copies, waits for them, and re-layouts  7.51 us (10%)
  other arithmetic  1.62 us (2%)
    pallas_call x1, Pallas kernels, sums_call(): pl.pallas_call(functools.partial(sums_kernel, count), out_shape=(jax.Shap...  37.5 us
    pallas_call x1, Pallas kernels, misfit_call(): pl.pallas_call(misfit_kernel, out_shape=(jax.ShapeDtypeStruct(low.shape,...  18.7 us
    pallas_call x1, Pallas kernels, border_call(): pl.pallas_call(functools.partial(border_kernel, count), out_shape=(side,...  9.97 us
    unnamed x10, local copies, waits for them, and re-layouts  6.11 us

profile of v2, /device:TPU:7, one launch (start us, length us, event | category | flops | bytes accessed | tf_op | source)
XLA Modules:
  0.0 76.0 jit_solution(7600880188005238404)
XLA Ops:
  0.6 0.1 add_convert_fusion
  0.7 0.1 pad_add_fusion
  0.8 1.2 %dynamic_slice.3 = s32[1]{0:T(128)} dynamic-slice(s32[16]{0:T(128)} %param.10, s32[]{:T(128)S(6)} %select_n.3), dynamic_slice_sizes={1} | dynamic-slice | bytes 12 | tf_op jit(solution)/shard_map/dynamic_slice | solution.py:392
  2.0 0.7 pad_add_fusion.1.count
  2.7 0.7 broadcast_subtract_fusion
  3.5 0.1 copy.9
  3.6 0.1 reshape.14.corner
  3.7 10.0 %border.1 = (f32[2,128,512]{2,1,0:T(8,128)}, f32[2,128,512]{2,1,0:T(8,128)}) custom-call(f32[2,256,512]{2,1,0:T(8,128)} %own.3), custom_call_target="tpu_custom_call" | custom-call | tf_op jit(solution)/shard_map/border/pallas_call | solution.py:237
  13.6 0.0 copy-start
  13.7 1.2 %copy-done = f32[2,256,512]{2,1,0:T(8,128)S(1)} copy-done((f32[2,256,512]{2,1,0:T(8,128)S(1)}, f32[2,256,512]{2,1,0:T(8,128)}, u32[]{:S(2)}) %copy-start) | copy-done | bytes 1048600
  14.9 0.0 copy-start.1
  14.9 1.0 %copy-done.1 = f32[2,256,256]{2,1,0:T(8,128)S(1)} copy-done((f32[2,256,256]{2,1,0:T(8,128)S(1)}, f32[2,256,256]{2,1,0:T(8,128)}, u32[]{:S(2)}) %copy-start.1) | copy-done | bytes 524312
  15.9 0.0 copy-start.2
  15.9 1.0 %copy-done.2 = f32[2,128,512]{2,1,0:T(8,128)S(1)} copy-done((f32[2,128,512]{2,1,0:T(8,128)S(1)}, f32[2,128,512]{2,1,0:T(8,128)}, u32[]{:S(2)}) %copy-start.2) | copy-done | bytes 524312
  17.0 0.0 copy-start.3
  17.0 1.0 %copy-done.3 = f32[2,128,512]{2,1,0:T(8,128)S(1)} copy-done((f32[2,128,512]{2,1,0:T(8,128)S(1)}, f32[2,128,512]{2,1,0:T(8,128)}, u32[]{:S(2)}) %copy-start.3) | copy-done | bytes 524312
  18.0 18.7 %misfit.1 = (f32[2,128,512]{2,1,0:T(8,128)S(1)}, f32[2,256,512]{2,1,0:T(8,128)S(1)}, f32[2,128,512]{2,1,0:T(8,128)S(1)}, f32[2,256,256]{2,1,0:T(8,128)S(1)}) custom-call(s32[16]{0:T(128)S(1)} %reshape.14.corner, s32[3]{0:T(128)S(1)} %pad_add_fusion.1.count, f32[2,128,512]{2,1,0:T(8,128)S(1)} %copy-done.2, f32[2,256,512]{2,1,0:T(8,128)S(1)} %copy-done, ...), custom_call_target="tpu_custom_call" | custom-call | tf_op jit(solution)/shard_map/misfit/pallas_call | solution.py:159
  36.7 37.5 %sums.1 = (f32[2,256,512]{2,1,0:T(8,128)S(1)}, f32[512,256]{1,0:T(8,128)S(1)}) custom-call(f32[2,128,512]{2,1,0:T(8,128)S(1)} %get-tuple-element.12.grad_low, f32[2,256,512]{2,1,0:T(8,128)S(1)} %get-tuple-element.13.grad_own, f32[2,128,512]{2,1,0:T(8,128)S(1)} %get-tuple-element.14.grad_high, f32[512,256]{1,0:T(8,128)S(1)} %bitcast.5), custom_call_target="tpu_custom_call" | custom-call | tf_op jit(solution)/shard_map/sums/pallas_call | solution.py:369
  74.2 1.0 %copy.12 = f32[2,256,512]{2,1,0:T(8,128)} copy(f32[2,256,512]{2,1,0:T(8,128)S(1)} %get-tuple-element.20) | data formatting | bytes 2097152
  75.2 0.8 %copy.13 = f32[2,256,256]{2,1,0:T(8,128)} copy(f32[2,256,256]{2,1,0:T(8,128)S(1)} %bitcast.6) | data formatting | bytes 1048576
Async XLA Ops:
  13.6 1.2 %copy-start = (f32[2,256,512]{2,1,0:T(8,128)S(1)}, f32[2,256,512]{2,1,0:T(8,128)}, u32[]{:S(2)}) copy-start(f32[2,256,512]{2,1,0:T(8,128)} %own.3) | copy-start | bytes 3145732
  14.9 1.0 %copy-start.1 = (f32[2,256,256]{2,1,0:T(8,128)S(1)}, f32[2,256,256]{2,1,0:T(8,128)}, u32[]{:S(2)}) copy-start(f32[2,256,256]{2,1,0:T(8,128)} %probe.1) | copy-start | bytes 1572868
  15.9 1.0 %copy-start.2 = (f32[2,128,512]{2,1,0:T(8,128)S(1)}, f32[2,128,512]{2,1,0:T(8,128)}, u32[]{:S(2)}) copy-start(f32[2,128,512]{2,1,0:T(8,128)} %get-tuple-element.10.low) | copy-start | bytes 1572868
  17.0 1.0 %copy-start.3 = (f32[2,128,512]{2,1,0:T(8,128)S(1)}, f32[2,128,512]{2,1,0:T(8,128)}, u32[]{:S(2)}) copy-start(f32[2,128,512]{2,1,0:T(8,128)} %get-tuple-element.11.high) | copy-start | bytes 1572868

commit v3 on v2

--- a/solution.py
+++ b/solution.py
@@ -12,6 +12,7 @@
 
 F32 = jnp.float32
 BF16 = jnp.bfloat16
+WIDTH = 2
 
 
 def tables(extent):
@@ -87,22 +88,19 @@
     return lanes(total[:, :h], other[:, :h]), lanes(total[:, h:], other[:, h:])
 
 
-def misfit_kernel(
-    corner, count, low, own, high, probe, patterns, table, grad_low, grad_own, grad_high, grad_probe, field, total, ordered
-):
+def misfit_kernel(positions, counts, field, probe, patterns, table, total, grad_probe, ordered):
     extent = probe.shape[1]
     h = extent // 2
-    tile = own.shape[1]
-    field[:, h : h + tile] = own[...]
-    field[:, :h] = jnp.where(count[1] > 0, low[...], jnp.zeros_like(low))
-    field[:, h + tile :] = jnp.where(count[2] > 0, high[...], jnp.zeros_like(high))
+    tile = field.shape[1] - extent
+    me = lax.axis_index("row")
+    live = counts[me]
     total[...] = jnp.zeros_like(total)
     grad_probe[...] = jnp.zeros_like(grad_probe)
     column = lax.broadcasted_iota(jnp.int32, (extent, extent), 1)
 
-    def step(slot, carry):
-        first = corner[2 * slot]
-        shift = corner[2 * slot + 1]
+    def load(slot):
+        first = positions[slot, 0] - (me * tile - h)
+        shift = positions[slot, 1]
         kept = column >= shift
         sub = lax.rem(first, 8)
         base = pl.multiple_of(first - sub, 8)
@@ -119,18 +117,26 @@
         turned = [
             pltpu.roll(pltpu.roll(probe[i], lax.rem(shift, extent), 1), sub, 0) for i in (0, 1)
         ]
+        return shift, kept, sub, at, after, inside, patch, turned
+
+    def gradient(slot, lane, patch, turned):
         even, odd = transform(
             turned[0] * patch[0] - turned[1] * patch[1], turned[0] * patch[1] + turned[1] * patch[0], table
         )
         permuted = dot(lanes(*parts(patterns[slot])), rows(table[8], table[8]))
-        ordered[0] = permuted[:, :h]
-        ordered[1] = permuted[:, h:]
+        ordered[lane, 0] = permuted[:, :h]
+        ordered[lane, 1] = permuted[:, h:]
+        alive = (slot < live).astype(F32)
         results = []
         for parity, value in ((0, even), (1, odd)):
-            pattern = lanes(ordered[0, pl.ds(parity, h, 2), :], ordered[1, pl.ds(parity, h, 2), :])
-            gap = value[:h] * value[:h] + value[h:] * value[h:] - pattern
+            picked = pl.ds(parity, h, 2)
+            pattern = lanes(ordered[lane, 0, picked, :], ordered[lane, 1, picked, :])
+            gap = (value[:h] * value[:h] + value[h:] * value[h:] - pattern) * alive
             results.append(rows(gap * value[:h], gap * value[h:]))
-        re, im = inverse(results[0], results[1], table)
+        return inverse(results[0], results[1], table)
+
+    def add(where, patch, turned, re, im):
+        shift, kept, sub, at, after, inside = where
         zero = jnp.zeros_like(re)
         grads = (turned[0] * re + turned[1] * im, turned[0] * im - turned[1] * re)
         for i in (0, 1):
@@ -144,33 +150,30 @@
         up = lax.rem(extent - sub, extent)
         for i, value in enumerate((patch[0] * re + patch[1] * im, patch[0] * im - patch[1] * re)):
             grad_probe[i] += pltpu.roll(pltpu.roll(value, back, 1), up, 0)
+
+    def step(group, carry):
+        slots = [group * WIDTH + lane for lane in range(WIDTH)]
+        loaded = [load(slot) for slot in slots]
+        grads = [gradient(slot, lane, *loaded[lane][6:]) for lane, slot in enumerate(slots)]
+        for one, (re, im) in zip(loaded, grads):
+            add(one[:6], one[6], one[7], re, im)
         return carry
 
-    lax.fori_loop(0, count[0], step, 0)
-    grad_low[...] = total[:, :h]
-    grad_own[...] = total[:, h : h + tile]
-    grad_high[...] = total[:, h + tile :]
-
-
-def misfit_call(corner, count, low, own, high, probe, patterns, table):
+    lax.fori_loop(0, (live + WIDTH - 1) // WIDTH, step, 0)
+
+
+def misfit_call(positions, counts, field, probe, patterns, table):
     vmem = pl.BlockSpec(memory_space=pltpu.VMEM)
     smem = pl.BlockSpec(memory_space=pltpu.SMEM)
-    height = low.shape[1] + own.shape[1] + high.shape[1]
     return pl.pallas_call(
         misfit_kernel,
-        out_shape=(
-            jax.ShapeDtypeStruct(low.shape, F32),
-            jax.ShapeDtypeStruct(own.shape, F32),
-            jax.ShapeDtypeStruct(high.shape, F32),
-            jax.ShapeDtypeStruct(probe.shape, F32),
-        ),
-        in_specs=[smem, smem] + [vmem] * 6,
-        out_specs=(vmem,) * 4,
-        scratch_shapes=[pltpu.VMEM((2, height, own.shape[2]), F32)] * 2
-        + [pltpu.VMEM((2, probe.shape[1], probe.shape[1] // 2), F32)],
-        compiler_params=pltpu.CompilerParams(vmem_limit_bytes=48 * 1024 * 1024),
+        out_shape=(jax.ShapeDtypeStruct(field.shape, F32), jax.ShapeDtypeStruct(probe.shape, F32)),
+        in_specs=[smem, smem] + [vmem] * 4,
+        out_specs=(vmem, vmem),
+        scratch_shapes=[pltpu.VMEM((WIDTH, 2, probe.shape[1], probe.shape[1] // 2), F32)],
+        compiler_params=pltpu.CompilerParams(vmem_limit_bytes=44 * 1024 * 1024),
         name="misfit",
-    )(corner, count, low, own, high, probe, patterns, table)
+    )(positions, counts, field, probe, patterns, table)
 
 
 def radices(count):
@@ -212,13 +215,26 @@
     return lax.min(me, 1) + lax.min(count - 1 - me, 1)
 
 
-def border_kernel(count, own, low, high, send, recv):
+def border_kernel(count, own, probe, patterns, table, field, probe_in, patterns_in, table_in, send, recv, here):
     me = lax.axis_index("row")
-    h = low.shape[1]
+    tile = own.shape[1]
+    h = (field.shape[1] - tile) // 2
     up, down = lax.max(me - 1, 0), lax.min(me + 1, count - 1)
+    low, high = field.at[:, :h], field.at[:, h + tile :]
+    moves = [
+        pltpu.make_async_copy(source, target, here.at[i])
+        for i, (source, target) in enumerate(
+            (
+                (own, field.at[:, h : h + tile]),
+                (probe, probe_in),
+                (patterns, patterns_in),
+                (table, table_in),
+            )
+        )
+    ]
     copies = (
         remote(own.at[:, :h], high, send.at[0], recv.at[1], up),
-        remote(own.at[:, own.shape[1] - h :], low, send.at[1], recv.at[0], down),
+        remote(own.at[:, tile - h :], low, send.at[1], recv.at[0], down),
     )
     arrivals = (
         remote(own.at[:, :h], low, send.at[0], recv.at[0], up),
@@ -227,28 +243,46 @@
     both_sides(me, count, lambda side: signal((up, down)[side]))
     pl.semaphore_wait(pltpu.get_barrier_semaphore(), neighbours(me, count))
     both_sides(me, count, lambda side: copies[side].start())
+    for move in moves:
+        move.start()
+
+    @pl.when(me == 0)
+    def _():
+        field[:, :h] = jnp.zeros((2, h, field.shape[2]), F32)
+
+    @pl.when(me == count - 1)
+    def _():
+        field[:, h + tile :] = jnp.zeros((2, h, field.shape[2]), F32)
+
+    for move in moves:
+        move.wait()
     both_sides(me, count, lambda side: arrivals[side].wait_recv())
     both_sides(me, count, lambda side: copies[side].wait_send())
 
 
-def border_call(own, h, count):
+def border_call(own, probe, patterns, table, h, count):
     anywhere = pl.BlockSpec(memory_space=pl.ANY)
-    side = jax.ShapeDtypeStruct((own.shape[0], h, own.shape[2]), F32)
+    vmem = pl.BlockSpec(memory_space=pltpu.VMEM)
+    field = jax.ShapeDtypeStruct((own.shape[0], own.shape[1] + 2 * h, own.shape[2]), F32)
+    same = [jax.ShapeDtypeStruct(value.shape, value.dtype) for value in (probe, patterns, table)]
     return pl.pallas_call(
         functools.partial(border_kernel, count),
-        out_shape=(side, side),
-        in_specs=[anywhere],
-        out_specs=(anywhere, anywhere),
-        scratch_shapes=[pltpu.SemaphoreType.DMA((2,)), pltpu.SemaphoreType.DMA((2,))],
-        compiler_params=pltpu.CompilerParams(collective_id=0, has_side_effects=True),
+        out_shape=(field, *same),
+        in_specs=[anywhere] * 4,
+        out_specs=(vmem,) * 4,
+        scratch_shapes=[pltpu.SemaphoreType.DMA((2,)), pltpu.SemaphoreType.DMA((2,)), pltpu.SemaphoreType.DMA((4,))],
+        compiler_params=pltpu.CompilerParams(
+            collective_id=0, has_side_effects=True, vmem_limit_bytes=40 * 1024 * 1024
+        ),
         name="border",
-    )(own)
-
-
-def sums_kernel(count, grad_low, grad_own, grad_high, probe, out, out_probe, from_above, from_below, *scratch):
+    )(own, probe, patterns, table)
+
+
+def sums_kernel(count, grads, probe, out, out_probe, from_above, from_below, *scratch):
     me = lax.axis_index("row")
-    h = grad_low.shape[1]
-    tile = grad_own.shape[1]
+    tile = out.shape[1]
+    h = from_above.shape[1]
+    grad_low, grad_high = grads.at[:, :h], grads.at[:, h + tile :]
     steps = radices(count)
     halo_send, halo_recv, rs_send, rs_recv, ag_send, ag_recv = scratch[:6]
     held = scratch[6 : 6 + len(steps)]
@@ -313,7 +347,7 @@
         for copy in copies:
             copy.start()
         started += copies
-        if depth == 0:
+        if depth == min(1, len(levels) - 1):
             both_sides(me, count, lambda side: halos[side].start())
         source = probe if depth == 0 else held[depth - 1]
         value = source[pl.ds(pl.multiple_of(digit * size, 8), size)]
@@ -344,7 +378,7 @@
             theirs = pl.ds(pl.multiple_of(first + other * size, 8), size)
             remote(out_probe.at[region], out_probe.at[theirs], ag_send.at[i], ag_recv.at[i], peer).wait_recv()
 
-    out[...] = grad_own[...]
+    out[...] = grads[:, h : h + tile]
 
     def add_side(side):
         arrivals[side].wait_recv()
@@ -357,7 +391,7 @@
     both_sides(me, count, lambda side: halos[side].wait_send())
 
 
-def sums_call(grad_low, grad_own, grad_high, probe, count):
+def sums_call(grads, probe, h, count):
     vmem = pl.BlockSpec(memory_space=pltpu.VMEM)
     steps = radices(count)
     pieces = sum(radix - 1 for radix in steps)
@@ -368,10 +402,10 @@
         landed.append(pltpu.VMEM((radix - 1, size, probe.shape[1]), F32))
     return pl.pallas_call(
         functools.partial(sums_kernel, count),
-        out_shape=(jax.ShapeDtypeStruct(grad_own.shape, F32), jax.ShapeDtypeStruct(probe.shape, F32)),
-        in_specs=[vmem] * 4,
+        out_shape=(jax.ShapeDtypeStruct((grads.shape[0], grads.shape[1] - 2 * h, grads.shape[2]), F32), jax.ShapeDtypeStruct(probe.shape, F32)),
+        in_specs=[vmem] * 2,
         out_specs=(vmem, vmem),
-        scratch_shapes=[pltpu.VMEM(grad_low.shape, F32)] * 2
+        scratch_shapes=[pltpu.VMEM((grads.shape[0], h, grads.shape[2]), F32)] * 2
         + [pltpu.SemaphoreType.DMA((2,))] * 2
         + [pltpu.SemaphoreType.DMA((pieces,))] * 4
         + held
@@ -380,25 +414,18 @@
             collective_id=1, has_side_effects=True, vmem_limit_bytes=40 * 1024 * 1024
         ),
         name="sums",
-    )(grad_low, grad_own, grad_high, probe)
+    )(grads, probe)
 
 
 def local(object_field, probe_wave, patterns, positions, counts):
-    tile = object_field.shape[1]
     extent = probe_wave.shape[1]
     h = extent // 2
-    me = lax.axis_index("row")
     size = lax.axis_size("row")
-    count = lax.dynamic_slice(counts, (me,), (1,))
-    low, high = border_call(object_field, h, size)
-    corner = (positions - jnp.stack([me * tile - h, 0 * me])[None]).reshape(-1)
-    setup = jnp.concatenate([count, jnp.stack([me > 0, me < size - 1]).astype(jnp.int32)])
     table = jnp.asarray(tables(extent))
-    grad_low, grad_own, grad_high, grad_probe = misfit_call(
-        corner, setup, low, object_field, high, probe_wave, patterns, table
-    )
-    grads, total = sums_call(grad_low, grad_own, grad_high, grad_probe.reshape(-1, extent), size)
-    return grads, total.reshape(grad_probe.shape)
+    field, probe, patterns, table = border_call(object_field, probe_wave, patterns, table, h, size)
+    grads, grad_probe = misfit_call(positions, counts, field, probe, patterns, table)
+    grads, grad_probe = sums_call(grads, grad_probe.reshape(-1, extent), h, size)
+    return grads, grad_probe.reshape(probe_wave.shape)
 
 
 def solution(mesh):

time: 76.8 us -> 70.3 us (0.915)
  the two profiles are of different devices: /device:TPU:7 before, /device:TPU:1 now
where the time goes in v3:
time: 70.3 us; the launch traced here: 69.6 us
  Pallas kernels  61.3 us (87%)
  local copies, waits for them, and re-layouts  7.65 us (11%)
    pallas_call x1, Pallas kernels, sums_call(): pl.pallas_call(functools.partial(sums_kernel, count), out_shape=(jax.Shap...  29.2 us
    pallas_call x1, Pallas kernels, misfit_call(): pl.pallas_call(misfit_kernel, out_shape=(jax.ShapeDtypeStruct(field.shape...  17.7 us
    pallas_call x1, Pallas kernels, border_call(): pl.pallas_call(functools.partial(border_kernel, count), out_shape=(field,...  14.4 us
    unnamed x13, local copies, waits for them, and re-layouts  7.65 us

profile of v3, /device:TPU:1, one launch (start us, length us, event | category | flops | bytes accessed | tf_op | source)
XLA Modules:
  0.0 69.6 jit_solution(8579353998414259290)
XLA Ops:
  0.6 0.8 %copy.8.positions = s32[8,2]{1,0:T(8,128)S(1)} copy(s32[8,2]{0,1:T(2,128)} %param.9) | data formatting | bytes 128 | tf_op args[3]
  1.4 0.0 copy-start
  1.4 1.6 %copy-done = f32[8,256,256]{2,1,0:T(8,128)S(1)} copy-done((f32[8,256,256]{2,1,0:T(8,128)S(1)}, f32[8,256,256]{2,1,0:T(8,128)}, u32[]{:S(2)}) %copy-start) | copy-done | bytes 2097176
  3.0 0.0 copy-start.1
  3.0 1.3 %copy-done.1 = bf16[9,256,256]{2,1,0:T(8,128)(2,1)S(1)} copy-done((bf16[9,256,256]{2,1,0:T(8,128)(2,1)S(1)}, bf16[9,256,256]{2,1,0:T(8,128)(2,1)}, u32[]{:S(2)}) %copy-start.1) | copy-done | bytes 1179672
  4.2 0.0 copy-start.2
  4.2 1.2 %copy-done.2 = f32[2,256,512]{2,1,0:T(8,128)S(1)} copy-done((f32[2,256,512]{2,1,0:T(8,128)S(1)}, f32[2,256,512]{2,1,0:T(8,128)}, u32[]{:S(2)}) %copy-start.2) | copy-done | bytes 1048600
  5.5 0.0 copy-start.3
  5.5 1.0 %copy-done.3 = f32[2,256,256]{2,1,0:T(8,128)S(1)} copy-done((f32[2,256,256]{2,1,0:T(8,128)S(1)}, f32[2,256,256]{2,1,0:T(8,128)}, u32[]{:S(2)}) %copy-start.3) | copy-done | bytes 524312
  6.5 0.0 copy-start.4
  6.5 14.4 %border.1 = (f32[2,512,512]{2,1,0:T(8,128)S(1)}, f32[2,256,256]{2,1,0:T(8,128)S(1)}, f32[8,256,256]{2,1,0:T(8,128)S(1)}, bf16[9,256,256]{2,1,0:T(8,128)(2,1)S(1)}) custom-call(f32[2,256,512]{2,1,0:T(8,128)S(1)} %copy-done.2, f32[2,256,256]{2,1,0:T(8,128)S(1)} %copy-done.3, f32[8,256,256]{2,1,0:T(8,128)S(1)} %copy-done, bf16[9,256,256]{2,1,0:T(8,128)(2,1)S(1)} %copy-done.1), custom_call_target="tpu_custom_call" | custom-call | tf_op jit(solution)/shard_map/border/pallas_call | solution.py:268
  21.0 0.0 copy-done.4
  21.0 17.7 %misfit.1 = (f32[2,512,512]{2,1,0:T(8,128)S(1)}, f32[2,256,256]{2,1,0:T(8,128)S(1)}) custom-call(s32[8,2]{1,0:T(8,128)S(1)} %copy.8.positions, s32[16]{0:T(128)S(1)} %copy-done.4, f32[2,512,512]{2,1,0:T(8,128)S(1)} %get-tuple-element.10.field, f32[2,256,256]{2,1,0:T(8,128)S(1)} %get-tuple-element.11.probe, f32[8,256,256]{2,1,0:T(8,128)S(1)} %get-tuple-element.12.patterns, ...), custom_call_target="tpu_custom_call" | custom-call | tf_op jit(solution)/shard_map/misfit/pallas_call | solution.py:168
  38.7 29.2 %sums.1 = (f32[2,256,512]{2,1,0:T(8,128)S(1)}, f32[512,256]{1,0:T(8,128)S(1)}) custom-call(f32[2,512,512]{2,1,0:T(8,128)S(1)} %get-tuple-element.14.grads, f32[512,256]{1,0:T(8,128)S(1)} %bitcast.2), custom_call_target="tpu_custom_call" | custom-call | tf_op jit(solution)/shard_map/sums/pallas_call | solution.py:403
  67.9 1.0 %copy.11 = f32[2,256,512]{2,1,0:T(8,128)} copy(f32[2,256,512]{2,1,0:T(8,128)S(1)} %get-tuple-element.20) | data formatting | bytes 2097152
  68.8 0.8 %copy.12 = f32[2,256,256]{2,1,0:T(8,128)} copy(f32[2,256,256]{2,1,0:T(8,128)S(1)} %bitcast.3) | data formatting | bytes 1048576
Async XLA Ops:
  1.4 1.6 %copy-start = (f32[8,256,256]{2,1,0:T(8,128)S(1)}, f32[8,256,256]{2,1,0:T(8,128)}, u32[]{:S(2)}) copy-start(f32[8,256,256]{2,1,0:T(8,128)} %patterns.1) | copy-start | bytes 6291460
  3.0 1.3 %copy-start.1 = (bf16[9,256,256]{2,1,0:T(8,128)(2,1)S(1)}, bf16[9,256,256]{2,1,0:T(8,128)(2,1)}, u32[]{:S(2)}) copy-start(bf16[9,256,256]{2,1,0:T(8,128)(2,1)} %constant.2.clone.table) | copy-start | bytes 3538948
  4.2 1.2 %copy-start.2 = (f32[2,256,512]{2,1,0:T(8,128)S(1)}, f32[2,256,512]{2,1,0:T(8,128)}, u32[]{:S(2)}) copy-start(f32[2,256,512]{2,1,0:T(8,128)} %own.1) | copy-start | bytes 3145732
  5.5 1.0 %copy-start.3 = (f32[2,256,256]{2,1,0:T(8,128)S(1)}, f32[2,256,256]{2,1,0:T(8,128)}, u32[]{:S(2)}) copy-start(f32[2,256,256]{2,1,0:T(8,128)} %probe.1) | copy-start | bytes 1572868
  6.5 14.5 %copy-start.4 = (s32[16]{0:T(128)S(1)}, s32[16]{0:T(128)}, u32[]{:S(2)}) copy-start(s32[16]{0:T(128)} %counts.1) | copy-start | bytes 196

commit v4 on v3

--- a/solution.py
+++ b/solution.py
@@ -88,6 +88,20 @@
     return lanes(total[:, :h], other[:, :h]), lanes(total[:, h:], other[:, h:])
 
 
+def turned_rows(value, amount, up):
+    groups = value.reshape(value.shape[0] // 8, 8, value.shape[1])
+    place = lax.broadcasted_iota(jnp.int32, groups.shape, 1)
+    if up:
+        inner = pltpu.roll(groups, lax.rem(8 - amount, 8), 1)
+        other = jnp.concatenate([inner[1:], inner[:1]], axis=0)
+        result = jnp.where(place < 8 - amount, inner, other)
+    else:
+        inner = pltpu.roll(groups, amount, 1)
+        other = jnp.concatenate([inner[-1:], inner[:-1]], axis=0)
+        result = jnp.where(place >= amount, inner, other)
+    return result.reshape(value.shape)
+
+
 def misfit_kernel(positions, counts, field, probe, patterns, table, total, grad_probe, ordered):
     extent = probe.shape[1]
     h = extent // 2
@@ -115,7 +129,7 @@
 
         patch = [patch_of(i) for i in (0, 1)]
         turned = [
-            pltpu.roll(pltpu.roll(probe[i], lax.rem(shift, extent), 1), sub, 0) for i in (0, 1)
+            turned_rows(pltpu.roll(probe[i], lax.rem(shift, extent), 1), sub, False) for i in (0, 1)
         ]
         return shift, kept, sub, at, after, inside, patch, turned
 
@@ -147,9 +161,8 @@
             total[i, after, :extent] += jnp.where(kept[:8], wrap, zero[:8])
             total[i, after, extent:] += jnp.where(kept[:8], zero[:8], wrap)
         back = lax.rem(extent - lax.rem(shift, extent), extent)
-        up = lax.rem(extent - sub, extent)
         for i, value in enumerate((patch[0] * re + patch[1] * im, patch[0] * im - patch[1] * re)):
-            grad_probe[i] += pltpu.roll(pltpu.roll(value, back, 1), up, 0)
+            grad_probe[i] += turned_rows(pltpu.roll(value, back, 1), sub, True)
 
     def step(group, carry):
         slots = [group * WIDTH + lane for lane in range(WIDTH)]
@@ -215,23 +228,13 @@
     return lax.min(me, 1) + lax.min(count - 1 - me, 1)
 
 
-def border_kernel(count, own, probe, patterns, table, field, probe_in, patterns_in, table_in, send, recv, here):
+def border_kernel(count, own, field, send, recv, here):
     me = lax.axis_index("row")
     tile = own.shape[1]
     h = (field.shape[1] - tile) // 2
     up, down = lax.max(me - 1, 0), lax.min(me + 1, count - 1)
     low, high = field.at[:, :h], field.at[:, h + tile :]
-    moves = [
-        pltpu.make_async_copy(source, target, here.at[i])
-        for i, (source, target) in enumerate(
-            (
-                (own, field.at[:, h : h + tile]),
-                (probe, probe_in),
-                (patterns, patterns_in),
-                (table, table_in),
-            )
-        )
-    ]
+    move = pltpu.make_async_copy(own, field.at[:, h : h + tile], here)
     copies = (
         remote(own.at[:, :h], high, send.at[0], recv.at[1], up),
         remote(own.at[:, tile - h :], low, send.at[1], recv.at[0], down),
@@ -243,8 +246,7 @@
     both_sides(me, count, lambda side: signal((up, down)[side]))
     pl.semaphore_wait(pltpu.get_barrier_semaphore(), neighbours(me, count))
     both_sides(me, count, lambda side: copies[side].start())
-    for move in moves:
-        move.start()
+    move.start()
 
     @pl.when(me == 0)
     def _():
@@ -254,28 +256,25 @@
     def _():
         field[:, h + tile :] = jnp.zeros((2, h, field.shape[2]), F32)
 
-    for move in moves:
-        move.wait()
+    move.wait()
     both_sides(me, count, lambda side: arrivals[side].wait_recv())
     both_sides(me, count, lambda side: copies[side].wait_send())
 
 
-def border_call(own, probe, patterns, table, h, count):
-    anywhere = pl.BlockSpec(memory_space=pl.ANY)
-    vmem = pl.BlockSpec(memory_space=pltpu.VMEM)
+def border_call(own, h, count):
     field = jax.ShapeDtypeStruct((own.shape[0], own.shape[1] + 2 * h, own.shape[2]), F32)
-    same = [jax.ShapeDtypeStruct(value.shape, value.dtype) for value in (probe, patterns, table)]
     return pl.pallas_call(
         functools.partial(border_kernel, count),
-        out_shape=(field, *same),
-        in_specs=[anywhere] * 4,
-        out_specs=(vmem,) * 4,
-        scratch_shapes=[pltpu.SemaphoreType.DMA((2,)), pltpu.SemaphoreType.DMA((2,)), pltpu.SemaphoreType.DMA((4,))],
+        out_shape=field,
+        in_specs=[pl.BlockSpec(memory_space=pl.ANY)],
+        out_specs=pl.BlockSpec(memory_space=pltpu.VMEM),
+        scratch_shapes=[pltpu.SemaphoreType.DMA((2,)), pltpu.SemaphoreType.DMA((2,)), pltpu.SemaphoreType.DMA],
         compiler_params=pltpu.CompilerParams(
-            collective_id=0, has_side_effects=True, vmem_limit_bytes=40 * 1024 * 1024
+            collective_id=0, has_side_effects=True, vmem_limit_bytes=16 * 1024 * 1024
         ),
+        cost_estimate=pl.CostEstimate(flops=10**10, bytes_accessed=8 * 1024 * 1024, transcendentals=0),
         name="border",
-    )(own, probe, patterns, table)
+    )(own)
 
 
 def sums_kernel(count, grads, probe, out, out_probe, from_above, from_below, *scratch):
@@ -349,6 +348,7 @@
         started += copies
         if depth == min(1, len(levels) - 1):
             both_sides(me, count, lambda side: halos[side].start())
+            out[...] = grads[:, h : h + tile]
         source = probe if depth == 0 else held[depth - 1]
         value = source[pl.ds(pl.multiple_of(digit * size, 8), size)]
         for k, arrival in enumerate(rs_arrivals(depth)):
@@ -377,8 +377,6 @@
         for i, k, other, peer in others:
             theirs = pl.ds(pl.multiple_of(first + other * size, 8), size)
             remote(out_probe.at[region], out_probe.at[theirs], ag_send.at[i], ag_recv.at[i], peer).wait_recv()
-
-    out[...] = grads[:, h : h + tile]
 
     def add_side(side):
         arrivals[side].wait_recv()
@@ -422,8 +420,8 @@
     h = extent // 2
     size = lax.axis_size("row")
     table = jnp.asarray(tables(extent))
-    field, probe, patterns, table = border_call(object_field, probe_wave, patterns, table, h, size)
-    grads, grad_probe = misfit_call(positions, counts, field, probe, patterns, table)
+    field = border_call(object_field, h, size)
+    grads, grad_probe = misfit_call(positions, counts, field, probe_wave, patterns, table)
     grads, grad_probe = sums_call(grads, grad_probe.reshape(-1, extent), h, size)
     return grads, grad_probe.reshape(probe_wave.shape)
 

time: 70.3 us -> 65.6 us (0.933); the launches traced: 69.6 us -> 65.9 us
  local copies, waits for them, and re-layouts: 7.65 us -> 3.76 us
    pallas_call x1, Pallas kernels: 29.2 us -> 42.3 us  [sums_call(): pl.pallas_call(functools.partial(sums_kernel, count), out_shape=(jax.Shap...]
    pallas_call x1, Pallas kernels: 17.7 us -> 4.65 us  [misfit_call(): pl.pallas_call(misfit_kernel, out_shape=(jax.ShapeDtypeStruct(field.shape...]
    unnamed x13, local copies, waits for them, and re-layouts: 7.65 us -> 3.76 us
where the time goes in v4:
time: 65.6 us; the launch traced here: 65.9 us
  Pallas kernels  61.4 us (94%)
  local copies, waits for them, and re-layouts  3.76 us (6%)
  between operations  0.69 us (1%)
    pallas_call x1, Pallas kernels, sums_call(): pl.pallas_call(functools.partial(sums_kernel, count), out_shape=(jax.Shap...  42.3 us
    pallas_call x1, Pallas kernels, border_call(): pl.pallas_call(functools.partial(border_kernel, count), out_shape=field,...  14.5 us
    pallas_call x1, Pallas kernels, misfit_call(): pl.pallas_call(misfit_kernel, out_shape=(jax.ShapeDtypeStruct(field.shape...  4.65 us
    unnamed x13, local copies, waits for them, and re-layouts  3.76 us

profile of v4, /device:TPU:1, one launch (start us, length us, event | category | flops | bytes accessed | tf_op | source)
XLA Modules:
  0.0 65.9 jit_solution(10534236368960387987)
XLA Ops:
  0.6 0.8 %copy.8.positions = s32[8,2]{1,0:T(8,128)S(1)} copy(s32[8,2]{0,1:T(2,128)} %param.9) | data formatting | bytes 128 | tf_op args[3]
  1.4 0.0 copy-start.4
  1.4 1.2 %copy-done.4 = f32[2,256,512]{2,1,0:T(8,128)S(1)} copy-done((f32[2,256,512]{2,1,0:T(8,128)S(1)}, f32[2,256,512]{2,1,0:T(8,128)}, u32[]{:S(2)}) %copy-start.4) | copy-done | bytes 1048600
  2.6 0.0 copy-start
  2.6 0.0 copy-start.1
  2.6 0.0 copy-start.2
  2.6 0.0 copy-start.3
  2.6 14.5 %border.1.field = f32[2,512,512]{2,1,0:T(8,128)S(1)} custom-call(f32[2,256,512]{2,1,0:T(8,128)S(1)} %copy-done.4), custom_call_target="tpu_custom_call" | custom-call | flops 10000000000 | bytes 8388608 | tf_op jit(solution)/shard_map/border/pallas_call | solution.py:266
  17.1 0.0 copy-done
  17.1 0.0 copy-done.1
  17.1 0.0 copy-done.2
  17.1 0.0 copy-done.3
  17.1 4.7 %misfit.1 = (f32[2,512,512]{2,1,0:T(8,128)S(1)}, f32[2,256,256]{2,1,0:T(8,128)S(1)}) custom-call(s32[8,2]{1,0:T(8,128)S(1)} %copy.8.positions, s32[16]{0:T(128)S(1)} %copy-done.3, f32[2,512,512]{2,1,0:T(8,128)S(1)} %border.1.field, f32[2,256,256]{2,1,0:T(8,128)S(1)} %copy-done.2, f32[8,256,256]{2,1,0:T(8,128)S(1)} %copy-done, bf16[9,256,256]{2,1,0:T(8,128)(2,1)S(1)} %copy-done.1), custom_call_target="tpu_custom_call" | custom-call | tf_op jit(solution)/shard_map/misfit/pallas_call | solution.py:181
  21.8 42.3 %sums.1 = (f32[2,256,512]{2,1,0:T(8,128)S(1)}, f32[512,256]{1,0:T(8,128)S(1)}) custom-call(f32[2,512,512]{2,1,0:T(8,128)S(1)} %get-tuple-element.6.grads, f32[512,256]{1,0:T(8,128)S(1)} %bitcast.2), custom_call_target="tpu_custom_call" | custom-call | tf_op jit(solution)/shard_map/sums/pallas_call | solution.py:401
  64.1 1.0 %copy.11 = f32[2,256,512]{2,1,0:T(8,128)} copy(f32[2,256,512]{2,1,0:T(8,128)S(1)} %get-tuple-element.12) | data formatting | bytes 2097152
  65.1 0.8 %copy.12 = f32[2,256,256]{2,1,0:T(8,128)} copy(f32[2,256,256]{2,1,0:T(8,128)S(1)} %bitcast.3) | data formatting | bytes 1048576
Async XLA Ops:
  1.4 1.2 %copy-start.4 = (f32[2,256,512]{2,1,0:T(8,128)S(1)}, f32[2,256,512]{2,1,0:T(8,128)}, u32[]{:S(2)}) copy-start(f32[2,256,512]{2,1,0:T(8,128)} %own.1) | copy-start | bytes 3145732
  2.6 14.5 %copy-start = (f32[8,256,256]{2,1,0:T(8,128)S(1)}, f32[8,256,256]{2,1,0:T(8,128)}, u32[]{:S(2)}) copy-start(f32[8,256,256]{2,1,0:T(8,128)} %patterns.1) | copy-start | bytes 6291460
  2.6 14.5 %copy-start.1 = (bf16[9,256,256]{2,1,0:T(8,128)(2,1)S(1)}, bf16[9,256,256]{2,1,0:T(8,128)(2,1)}, u32[]{:S(2)}) copy-start(bf16[9,256,256]{2,1,0:T(8,128)(2,1)} %constant.2.clone.table) | copy-start | bytes 3538948
  2.6 14.5 %copy-start.2 = (f32[2,256,256]{2,1,0:T(8,128)S(1)}, f32[2,256,256]{2,1,0:T(8,128)}, u32[]{:S(2)}) copy-start(f32[2,256,256]{2,1,0:T(8,128)} %probe.1) | copy-start | bytes 1572868
  2.6 14.5 %copy-start.3 = (s32[16]{0:T(128)S(1)}, s32[16]{0:T(128)}, u32[]{:S(2)}) copy-start(s32[16]{0:T(128)} %counts.1) | copy-start | bytes 196

commit v5 on v4

--- a/solution.py
+++ b/solution.py
@@ -12,7 +12,8 @@
 
 F32 = jnp.float32
 BF16 = jnp.bfloat16
-WIDTH = 2
+WIDTH = 4
+PIECES = 4
 
 
 def tables(extent):
@@ -309,14 +310,30 @@
             signal(peer)
     pl.semaphore_wait(pltpu.get_barrier_semaphore(), index + neighbours(me, count))
 
-    halos = (
-        remote(grad_low, from_below, halo_send.at[0], halo_recv.at[1], up),
-        remote(grad_high, from_above, halo_send.at[1], halo_recv.at[0], down),
-    )
-    arrivals = (
-        remote(grad_low, from_above, halo_send.at[0], halo_recv.at[0], up),
-        remote(grad_high, from_below, halo_send.at[1], halo_recv.at[1], down),
-    )
+    part = h // PIECES
+
+    def piece(ref, k):
+        return ref.at[:, k * part : (k + 1) * part]
+
+    halos, arrivals = [], []
+    for k in range(PIECES):
+        low, high = piece(grad_low, k), piece(grad_high, k)
+        above, below = piece(from_above, k), piece(from_below, k)
+        halos.append(
+            (
+                remote(low, below, halo_send.at[0, k], halo_recv.at[1, k], up),
+                remote(high, above, halo_send.at[1, k], halo_recv.at[0, k], down),
+            )
+        )
+        arrivals.append(
+            (
+                remote(low, above, halo_send.at[0, k], halo_recv.at[0, k], up),
+                remote(high, below, halo_send.at[1, k], halo_recv.at[1, k], down),
+            )
+        )
+
+    def send_halo(k):
+        both_sides(me, count, lambda side: halos[k][side].start())
 
     def rs_copies(depth):
         radix, digit, size, _, others = levels[depth]
@@ -341,13 +358,16 @@
         ]
 
     started = []
+    sent = 0
     for depth, (radix, digit, size, _, others) in enumerate(levels):
         copies = rs_copies(depth)
         for copy in copies:
             copy.start()
         started += copies
-        if depth == min(1, len(levels) - 1):
-            both_sides(me, count, lambda side: halos[side].start())
+        if depth >= 1 and sent < PIECES:
+            send_halo(sent)
+            sent += 1
+        if depth == 0:
             out[...] = grads[:, h : h + tile]
         source = probe if depth == 0 else held[depth - 1]
         value = source[pl.ds(pl.multiple_of(digit * size, 8), size)]
@@ -374,19 +394,26 @@
         for copy in copies:
             copy.start()
         started += copies
+        while sent < PIECES:
+            send_halo(sent)
+            sent += 1
+            if depth > 1:
+                break
         for i, k, other, peer in others:
             theirs = pl.ds(pl.multiple_of(first + other * size, 8), size)
             remote(out_probe.at[region], out_probe.at[theirs], ag_send.at[i], ag_recv.at[i], peer).wait_recv()
 
     def add_side(side):
-        arrivals[side].wait_recv()
+        for k in range(PIECES):
+            arrivals[k][side].wait_recv()
         where, value = ((slice(0, h), from_above), (slice(tile - h, tile), from_below))[side]
         out[:, where] += value[...]
 
     both_sides(me, count, add_side)
     for copy in started:
         copy.wait_send()
-    both_sides(me, count, lambda side: halos[side].wait_send())
+    for k in range(PIECES):
+        both_sides(me, count, lambda side: halos[k][side].wait_send())
 
 
 def sums_call(grads, probe, h, count):
@@ -404,7 +431,7 @@
         in_specs=[vmem] * 2,
         out_specs=(vmem, vmem),
         scratch_shapes=[pltpu.VMEM((grads.shape[0], h, grads.shape[2]), F32)] * 2
-        + [pltpu.SemaphoreType.DMA((2,))] * 2
+        + [pltpu.SemaphoreType.DMA((2, PIECES))] * 2
         + [pltpu.SemaphoreType.DMA((pieces,))] * 4
         + held
         + landed,

time: 65.6 us -> 61.4 us (0.936); the launches traced: 65.9 us -> 61 us
  Pallas kernels: 61.4 us -> 56.6 us
    pallas_call x1, Pallas kernels: 42.3 us -> 26.4 us  [sums_call(): pl.pallas_call(functools.partial(sums_kernel, count), out_shape=(jax.Shap...]
    pallas_call x1, Pallas kernels: 4.65 us -> 15.7 us  [misfit_call(): pl.pallas_call(misfit_kernel, out_shape=(jax.ShapeDtypeStruct(field.shape...]
where the time goes in v5:
time: 61.4 us; the launch traced here: 61 us
  Pallas kernels  56.6 us (92%)
  local copies, waits for them, and re-layouts  3.76 us (6%)
  between operations  0.69 us (1%)
    pallas_call x1, Pallas kernels, sums_call(): pl.pallas_call(functools.partial(sums_kernel, count), out_shape=(jax.Shap...  26.4 us
    pallas_call x1, Pallas kernels, misfit_call(): pl.pallas_call(misfit_kernel, out_shape=(jax.ShapeDtypeStruct(field.shape...  15.7 us
    pallas_call x1, Pallas kernels, border_call(): pl.pallas_call(functools.partial(border_kernel, count), out_shape=field,...  14.5 us
    unnamed x13, local copies, waits for them, and re-layouts  3.76 us

profile of v5, /device:TPU:1, one launch (start us, length us, event | category | flops | bytes accessed | tf_op | source)
XLA Modules:
  0.0 61.0 jit_solution(10430018075371717327)
XLA Ops:
  0.6 0.8 %copy.8.positions = s32[8,2]{1,0:T(8,128)S(1)} copy(s32[8,2]{0,1:T(2,128)} %param.9) | data formatting | bytes 128 | tf_op args[3]
  1.4 0.0 copy-start.4
  1.4 1.2 %copy-done.4 = f32[2,256,512]{2,1,0:T(8,128)S(1)} copy-done((f32[2,256,512]{2,1,0:T(8,128)S(1)}, f32[2,256,512]{2,1,0:T(8,128)}, u32[]{:S(2)}) %copy-start.4) | copy-done | bytes 1048600
  2.6 0.0 copy-start
  2.6 0.0 copy-start.1
  2.6 0.0 copy-start.2
  2.6 0.0 copy-start.3
  2.6 14.5 %border.1.field = f32[2,512,512]{2,1,0:T(8,128)S(1)} custom-call(f32[2,256,512]{2,1,0:T(8,128)S(1)} %copy-done.4), custom_call_target="tpu_custom_call" | custom-call | flops 10000000000 | bytes 8388608 | tf_op jit(solution)/shard_map/border/pallas_call | solution.py:267
  17.1 0.0 copy-done
  17.1 0.0 copy-done.1
  17.1 0.0 copy-done.2
  17.1 0.0 copy-done.3
  17.1 15.7 %misfit.1 = (f32[2,512,512]{2,1,0:T(8,128)S(1)}, f32[2,256,256]{2,1,0:T(8,128)S(1)}) custom-call(s32[8,2]{1,0:T(8,128)S(1)} %copy.8.positions, s32[16]{0:T(128)S(1)} %copy-done.3, f32[2,512,512]{2,1,0:T(8,128)S(1)} %border.1.field, f32[2,256,256]{2,1,0:T(8,128)S(1)} %copy-done.2, f32[8,256,256]{2,1,0:T(8,128)S(1)} %copy-done, bf16[9,256,256]{2,1,0:T(8,128)(2,1)S(1)} %copy-done.1), custom_call_target="tpu_custom_call" | custom-call | tf_op jit(solution)/shard_map/misfit/pallas_call | solution.py:182
  32.9 26.4 %sums.1 = (f32[2,256,512]{2,1,0:T(8,128)S(1)}, f32[512,256]{1,0:T(8,128)S(1)}) custom-call(f32[2,512,512]{2,1,0:T(8,128)S(1)} %get-tuple-element.6.grads, f32[512,256]{1,0:T(8,128)S(1)} %bitcast.2), custom_call_target="tpu_custom_call" | custom-call | tf_op jit(solution)/shard_map/sums/pallas_call | solution.py:428
  59.2 1.0 %copy.11 = f32[2,256,512]{2,1,0:T(8,128)} copy(f32[2,256,512]{2,1,0:T(8,128)S(1)} %get-tuple-element.12) | data formatting | bytes 2097152
  60.2 0.8 %copy.12 = f32[2,256,256]{2,1,0:T(8,128)} copy(f32[2,256,256]{2,1,0:T(8,128)S(1)} %bitcast.3) | data formatting | bytes 1048576
Async XLA Ops:
  1.4 1.2 %copy-start.4 = (f32[2,256,512]{2,1,0:T(8,128)S(1)}, f32[2,256,512]{2,1,0:T(8,128)}, u32[]{:S(2)}) copy-start(f32[2,256,512]{2,1,0:T(8,128)} %own.1) | copy-start | bytes 3145732
  2.6 14.5 %copy-start = (f32[8,256,256]{2,1,0:T(8,128)S(1)}, f32[8,256,256]{2,1,0:T(8,128)}, u32[]{:S(2)}) copy-start(f32[8,256,256]{2,1,0:T(8,128)} %patterns.1) | copy-start | bytes 6291460
  2.6 14.5 %copy-start.1 = (bf16[9,256,256]{2,1,0:T(8,128)(2,1)S(1)}, bf16[9,256,256]{2,1,0:T(8,128)(2,1)}, u32[]{:S(2)}) copy-start(bf16[9,256,256]{2,1,0:T(8,128)(2,1)} %constant.2.clone.table) | copy-start | bytes 3538948
  2.6 14.5 %copy-start.2 = (f32[2,256,256]{2,1,0:T(8,128)S(1)}, f32[2,256,256]{2,1,0:T(8,128)}, u32[]{:S(2)}) copy-start(f32[2,256,256]{2,1,0:T(8,128)} %probe.1) | copy-start | bytes 1572868
  2.6 14.5 %copy-start.3 = (s32[16]{0:T(128)S(1)}, s32[16]{0:T(128)}, u32[]{:S(2)}) copy-start(s32[16]{0:T(128)} %counts.1) | copy-start | bytes 196
